TPU v7x, 512 devices: a whole 4x8x8 slice. The times are simulated.
512 devices in a mesh: gx: 8 (over y), gy: 4 (over x), gz: 16 (over z, core).
Axes of the slice: x: 4, y: 8, z: 8, core: 2. Of those that a mesh axis runs over, the one named last changes fastest.
Arguments:
- source: float32 [256, 256, 512], P('gz', 'gx', 'gy'), may hold values from -6 to 6
- conductivity: float32 [256, 256, 512], P('gz', 'gx', 'gy'), may hold values from 0.25 to 4
Outputs:
- correction: float32 [256, 256, 512], P('gz', 'gx', 'gy')
- residual: float32 [256, 256, 512], P('gz', 'gx', 'gy')
All inputs are finite; a program needn't handle non-finite values.
Results may differ from a plain program's by a relative error of at most 0.0003.
Values sent between devices are 32-bit elements; how exact they have to be, the bound alone decides.
A program may use at most 128 MiB of HBM per device.

v0:
```python
import jax
import jax.numpy as jnp
from jax import lax
from jax.sharding import PartitionSpec as P

LEVELS = 7
BOTTOM = 8


OMEGA = 2.0 / 3.0


def from_partner(x, axis, distance):
    return lax.ppermute(x, axis, [(i, i ^ 1 << distance) for i in range(lax.axis_size(axis))])


def padded(x, sides, width):
    for axis, dim in sides:
        devices, length = (lax.axis_size(axis), x.shape[dim])
        up = [(i, (i + 1) % devices) for i in range(devices - 1)]
        down = [(j, i) for i, j in up]
        last = lax.slice_in_dim(x, length - width, length, axis=dim)
        first = lax.slice_in_dim(x, 0, width, axis=dim)
        before = lax.ppermute(last, axis, up)
        after = lax.ppermute(first, axis, down)
        x = jnp.concatenate([before, x, after], axis=dim)
    return x


def crop(field, margin):
    return field[margin:-margin, margin:-margin, margin:-margin]


def neighbour_bounds(extent, dimension, offset):
    starts = [1, 1, 1]
    starts[dimension] = offset
    limits = [starts[0] + extent[0], starts[1] + extent[1], starts[2] + extent[2]]
    return (starts, limits)


def operate(field, weights, scale):
    centre = crop(field, 1)
    inner = crop(weights, 1)
    extent = centre.shape
    total = jnp.zeros_like(centre)
    diagonal = jnp.zeros_like(centre)
    for dimension in range(3):
        for offset in (0, 2):
            starts, limits = neighbour_bounds(extent, dimension, offset)
            neighbour = lax.slice(field, starts, limits)
            weight_near = lax.slice(weights, starts, limits)
            flux_weight = 0.5 * (inner + weight_near)
            total = total + flux_weight * (centre - neighbour)
            diagonal = diagonal + flux_weight
    return (scale * total, scale * diagonal)


def face_set(weights):
    inner = crop(weights, 1)
    extent = inner.shape
    fluxes = []
    diagonal = jnp.zeros_like(inner)
    for dimension in range(3):
        for offset in (0, 2):
            starts, limits = neighbour_bounds(extent, dimension, offset)
            flux_weight = 0.5 * (inner + lax.slice(weights, starts, limits))
            fluxes.append(flux_weight)
            diagonal = diagonal + flux_weight
    return (fluxes, diagonal)


def apply_faces(field, fluxes, scale):
    centre = crop(field, 1)
    extent = centre.shape
    total = jnp.zeros_like(centre)
    position = 0
    for dimension in range(3):
        for offset in (0, 2):
            starts, limits = neighbour_bounds(extent, dimension, offset)
            total = total + fluxes[position] * (centre - lax.slice(field, starts, limits))
            position = position + 1
    return scale * total


def relax_faces(field, source, fluxes, diagonal, scale):
    applied = apply_faces(field, fluxes, scale)
    scaled = scale * diagonal
    safe = jnp.where(scaled > 0.0, scaled, 1.0)
    return crop(field, 1) + OMEGA * (source - applied) / safe


def relax(field, source, weights, scale):
    applied, diagonal = operate(field, weights, scale)
    safe = jnp.where(diagonal > 0.0, diagonal, 1.0)
    updated = crop(field, 1) + OMEGA * (source - applied) / safe
    return updated


def restrict(block):
    layers, rows_count, columns = block.shape
    return (
        block.reshape(layers // 2, 2, rows_count // 2, 2, columns // 2, 2).sum(axis=(1, 3, 5))
        * 0.125
    )


def prolong(block):
    return jnp.repeat(jnp.repeat(jnp.repeat(block, 2, 0), 2, 1), 2, 2)


def cycle(source, weights, level):
    scale = 0.25**level
    wide_weight = jnp.pad(weights, 1)
    field = jnp.zeros_like(source)
    if level == LEVELS - 1:
        for sweep in range(BOTTOM):
            field = relax(jnp.pad(field, 1), source, wide_weight, scale)
        return field
    field = relax(jnp.pad(field, 1), source, wide_weight, scale)
    applied = operate(jnp.pad(field, 1), wide_weight, scale)[0]
    coarse = cycle(restrict(source - applied), restrict(weights), level + 1)
    field = field + prolong(coarse)
    field = relax(jnp.pad(field, 1), source, wide_weight, scale)
    return field


def combine_halves(pieces, partner, high_half, dimension):
    joined = []
    for own_part, peer_part in zip(pieces, partner):
        joined.append(
            jnp.where(
                high_half,
                jnp.concatenate([peer_part, own_part], dimension),
                jnp.concatenate([own_part, peer_part], dimension),
            )
        )
    return tuple(joined)


def gather_bricks(source_brick, weight_brick):
    pieces = (source_brick, weight_brick)
    for bit_number in range(lax.axis_size("gx").bit_length() - 1):
        partner = from_partner((pieces[0], pieces[1]), "gx", bit_number)
        pieces = combine_halves(pieces, partner, lax.axis_index("gx") >> bit_number & 1 == 1, 1)
    for bit_number in range(lax.axis_size("gy").bit_length() - 1):
        partner = from_partner((pieces[0], pieces[1]), "gy", bit_number)
        pieces = combine_halves(pieces, partner, lax.axis_index("gy") >> bit_number & 1 == 1, 2)
    for bit_number in range(lax.axis_size("gz").bit_length() - 1):
        partner = from_partner((pieces[0], pieces[1]), "gz", bit_number)
        pieces = combine_halves(pieces, partner, lax.axis_index("gz") >> bit_number & 1 == 1, 0)
    return pieces


def solve_merged(source_brick, weight_brick, level):
    full_source, full_weight = gather_bricks(source_brick, weight_brick)
    whole = cycle(full_source, full_weight, level)
    extent = source_brick.shape
    starts = (
        lax.axis_index("gz") * extent[0],
        lax.axis_index("gx") * extent[1],
        lax.axis_index("gy") * extent[2],
    )
    return lax.dynamic_slice(whole, starts, extent)


def body(source, conductivity):
    bottom_level = 4
    weights = [conductivity]
    for level in range(bottom_level):
        weights.append(restrict(weights[-1]))
    sources = [source]
    fields = []
    face_sets = []
    for level in range(bottom_level):
        ghost = padded(weights[level], (("gx", 1), ("gy", 2), ("gz", 0)), 1)
        face_sets.append(face_set(ghost))
    for level in range(bottom_level):
        scale = 0.25**level
        fluxes, diagonal = face_sets[level]
        empty = jnp.zeros(sources[level].shape, jnp.float32)
        field = relax_faces(jnp.pad(empty, 1), sources[level], fluxes, diagonal, scale)
        wide = padded(field, (("gx", 1), ("gy", 2), ("gz", 0)), 1)
        applied = apply_faces(wide, fluxes, scale)
        fields.append(field)
        sources.append(restrict(sources[level] - applied))
    coarse = solve_merged(sources[bottom_level], weights[bottom_level], bottom_level)
    for level in reversed(range(bottom_level)):
        fluxes, diagonal = face_sets[level]
        field = fields[level] + prolong(coarse)
        wide = padded(field, (("gx", 1), ("gy", 2), ("gz", 0)), 1)
        field = relax_faces(wide, sources[level], fluxes, diagonal, 0.25**level)
        coarse = field
    wide = padded(coarse, (("gx", 1), ("gy", 2), ("gz", 0)), 1)
    applied = apply_faces(wide, face_sets[0][0], 1.0)
    return (coarse, source - applied)


def solution(mesh):
    in_specs = (P("gz", "gx", "gy"), P("gz", "gx", "gy"))
    out_specs = (P("gz", "gx", "gy"), P("gz", "gx", "gy"))
    return jax.shard_map(body, mesh=mesh, in_specs=in_specs, out_specs=out_specs, check_vma=False)
```

profile of v0, /device:TPU:1, one launch (start us, length us, event | category | flops | bytes accessed | tf_op | source)
XLA Modules:
  0.0 518.4 jit_solution(6423847101057846691)
XLA Ops:
  1.5 4.0 collective-permute-start
  6.9 18.9 %reshape.1148 = f32[8,2,16,2,64,2]{5,4,3,2,1,0:T(8,128)} reshape(f32[16,32,128]{2,1,0:T(8,128)} %param.3) | data formatting | bytes 524288 | tf_op jit(solution)/shard_map/reshape | solution.py:102
  25.7 7.0 %reduce_sum.123 = f32[8,16,64]{2,1,0:T(8,128)S(1)} reduce(f32[8,2,16,2,64,2]{5,4,3,2,1,0:T(8,128)} %reshape.1148, f32[]{:T(128)} %constant.24.clone.1), dimensions={1,3,5}, to_apply=%region_1.0 | reduce | flops 57344 | bytes 294916 | tf_op jit(solution)/shard_map/reduce_sum | solution.py:102
  42.9 4.3 collective-permute-start.57
  62.2 5.8 %collective-permute-start.58 = (f32[1,4,8]{2,1,0:T(4,128)S(1)}, f32[1,4,8]{2,1,0:T(4,128)S(1)}, u32[]{:S(2)}, u32[]{:S(2)}) collective-permute-start(f32[1,4,8]{2,1,0:T(4,128)S(1)} %maximum_select_fusion.24), channel_id=1, source_target_pairs={{0,128},{64,192},{128,0},{192,64},{256,384},{320,448},{384,256},{4... | collective-permute-start | bytes 392 | tf_op jit(solution)/shard_map/ppermute | solution.py:14
  68.9 5.1 collective-permute-start.59
  94.2 15.2 %collective-permute-start.40 = (f32[1,6,18]{2,1,0:T(8,128)}, f32[1,6,18]{2,1,0:T(8,128)}, u32[]{:S(2)}, u32[]{:S(2)}) collective-permute-start(f32[1,6,18]{2,1,0:T(8,128)} %get-tuple-element.121), channel_id=1, source_target_pairs={{0,1},{1,2},{2,3},{3,4},{4,5},{5,6},{6,7},{7,8},{8,9},{9,10},{10,1... | collective-permute-start | bytes 1304 | tf_op jit(solution)/shard_map/ppermute | solution.py:24
  114.2 4.6 collective-permute-done.2
  118.7 4.1 collective-permute-done.3
  147.0 5.9 %collective-permute-start.16 = (f32[1,18,66]{2,0,1:T(1,128)S(1)}, f32[1,18,66]{2,0,1:T(1,128)S(1)}, u32[]{:S(2)}, u32[]{:S(2)}) collective-permute-start(f32[1,18,66]{2,0,1:T(1,128)S(1)} %get-tuple-element.79), channel_id=1, source_target_pairs={{0,1},{1,2},{2,3},{3,4},{4,5},{5,6},{6,7},{7,8},{8,9},{9,10},{10,1... | collective-permute-start | bytes 14264 | tf_op jit(solution)/shard_map/ppermute | solution.py:24
  156.3 5.4 %collective-permute-start.10 = (f32[1,34,130]{2,1,0:T(8,128)S(1)}, f32[1,34,130]{2,1,0:T(8,128)S(1)}, u32[]{:S(2)}, u32[]{:S(2)}) collective-permute-start(f32[1,34,130]{2,1,0:T(8,128)S(1)} %get-tuple-element.42), channel_id=1, source_target_pairs={{0,1},{1,2},{2,3},{3,4},{4,5},{5,6},{6,7},{7,8},{8,9},{9,10},{10,1... | collective-permute-start | bytes 53048 | tf_op jit(solution)/shard_map/ppermute | solution.py:24
  170.3 18.1 %reshape.1147 = f32[8,2,16,2,64,2]{5,4,3,2,1,0:T(8,128)} reshape(f32[16,32,128]{2,1,0:T(8,128)S(1)} %fusion.62) | data formatting | bytes 524288 | tf_op jit(solution)/shard_map/reshape | solution.py:102
  188.4 7.0 %reduce_sum.122 = f32[8,16,64]{2,1,0:T(8,128)S(1)} reduce(f32[8,2,16,2,64,2]{5,4,3,2,1,0:T(8,128)} %reshape.1147, f32[]{:T(128)} %constant.24.clone.1), dimensions={1,3,5}, to_apply=%region_0.0 | reduce | flops 57344 | bytes 294916 | tf_op jit(solution)/shard_map/reduce_sum | solution.py:102
  214.9 5.3 %collective-permute-start.22 = (f32[1,18,66]{2,0,1:T(1,128)S(1)}, f32[1,18,66]{2,0,1:T(1,128)S(1)}, u32[]{:S(2)}, u32[]{:S(2)}) collective-permute-start(f32[1,18,66]{2,0,1:T(1,128)S(1)} %get-tuple-element.72), channel_id=1, source_target_pairs={{0,1},{1,2},{2,3},{3,4},{4,5},{5,6},{6,7},{7,8},{8,9},{9,10},{10,1... | collective-permute-start | bytes 14264 | tf_op jit(solution)/shard_map/ppermute | solution.py:24
  230.8 4.9 collective-permute-start.30
  237.9 4.1 collective-permute-start.63
  242.1 4.2 collective-permute-start.32
  251.0 4.7 collective-permute-start.34
  267.7 10.9 %collective-permute-start.64 = (f32[4,16,32]{2,1,0:T(8,128)S(1)}, f32[4,16,32]{2,1,0:T(8,128)S(1)}, u32[]{:S(2)}, u32[]{:S(2)}) collective-permute-start(f32[4,16,32]{2,1,0:T(8,128)S(1)} %maximum_select_fusion.5), channel_id=1, source_target_pairs={{0,4},{1,5},{2,6},{3,7},{4,0},{5,1},{6,2},{7,3},{8,12},{9,13},{10,... | collective-permute-start | bytes 24584 | tf_op jit(solution)/shard_map/ppermute | solution.py:14
  286.4 4.4 collective-permute-start.46
  296.8 4.3 collective-permute-start.48
  301.1 5.6 %collective-permute-start.65 = (f32[8,16,32]{2,1,0:T(8,128)S(1)}, f32[8,16,32]{2,1,0:T(8,128)S(1)}, u32[]{:S(2)}, u32[]{:S(2)}) collective-permute-start(f32[8,16,32]{2,1,0:T(8,128)S(1)} %maximum_select_fusion.3), channel_id=1, source_target_pairs={{0,8},{1,9},{2,10},{3,11},{4,12},{5,13},{6,14},{7,15},{8,0},{9,1},... | collective-permute-start | bytes 49160 | tf_op jit(solution)/shard_map/ppermute | solution.py:14
  306.8 6.7 %collective-permute-start.49 = (f32[1,4,8]{2,1,0:T(4,128)S(1)}, f32[1,4,8]{2,1,0:T(4,128)S(1)}, u32[]{:S(2)}, u32[]{:S(2)}) collective-permute-start(f32[1,4,8]{2,1,0:T(4,128)S(1)} %maximum_select_fusion.22), channel_id=1, source_target_pairs={{0,128},{64,192},{128,0},{192,64},{256,384},{320,448},{384,256},{4... | collective-permute-start | bytes 392 | tf_op jit(solution)/shard_map/ppermute | solution.py:14
  318.4 4.4 collective-permute-done.50
  333.2 7.6 %collective-permute-start.53 = (f32[1,16,32]{2,1,0:T(8,128)S(1)}, f32[1,16,32]{2,1,0:T(8,128)S(1)}, u32[]{:S(2)}, u32[]{:S(2)}) collective-permute-start(f32[1,16,32]{2,1,0:T(8,128)S(1)} %maximum_select_fusion.12), channel_id=1, source_target_pairs={{0,1},{1,0},{2,3},{3,2},{4,5},{5,4},{6,7},{7,6},{8,9},{9,8},{10,11... | collective-permute-start | bytes 6152 | tf_op jit(solution)/shard_map/ppermute | solution.py:14
  357.5 6.1 %collective-permute-done.56 = f32[8,16,32]{2,1,0:T(8,128)S(1)} collective-permute-done((f32[8,16,32]{2,1,0:T(8,128)S(1)}, f32[8,16,32]{2,1,0:T(8,128)S(1)}, u32[]{:S(2)}, u32[]{:S(2)}) %collective-permute-start.56) | collective-permute-done | bytes 16416 | tf_op jit(solution)/shard_map/ppermute | solution.py:14
  380.6 4.1 collective-permute-done.67
  391.9 9.2 %collective-permute-start.70 = (f32[1,6,18]{2,1,0:T(8,128)S(1)}, f32[1,6,18]{2,1,0:T(8,128)S(1)}, u32[]{:S(2)}, u32[]{:S(2)}) collective-permute-start(f32[1,6,18]{2,1,0:T(8,128)S(1)} %get-tuple-element.112), channel_id=1, source_target_pairs={{0,1},{1,2},{2,3},{3,4},{4,5},{5,6},{6,7},{7,8},{8,9},{9,10},{10,1... | collective-permute-start | bytes 1304 | tf_op jit(solution)/shard_map/ppermute | solution.py:24
  420.8 4.8 collective-permute-start.76
  466.5 6.2 %collective-permute-done.86 = f32[16,34,1]{2,1,0:T(8,128)S(1)} collective-permute-done((f32[16,34,1]{2,1,0:T(8,128)S(1)}, f32[16,34,1]{2,1,0:T(8,128)S(1)}, u32[]{:S(2)}, u32[]{:S(2)}) %collective-permute-start.86) | collective-permute-done | bytes 2208 | tf_op jit(solution)/shard_map/ppermute | solution.py:24
  497.8 5.9 %collective-permute-done.92 = f32[16,34,1]{2,1,0:T(8,128)S(1)} collective-permute-done((f32[16,34,1]{2,1,0:T(8,128)S(1)}, f32[16,34,1]{2,1,0:T(8,128)S(1)}, u32[]{:S(2)}, u32[]{:S(2)}) %collective-permute-start.92) | collective-permute-done | bytes 2208 | tf_op jit(solution)/shard_map/ppermute | solution.py:24
  503.7 4.4 collective-permute-done.93
  (555 shorter events, 301.6 us)
Async XLA Ops:
  1.5 107.9 %collective-permute-start = (f32[16,1,128]{2,0,1:T(8,128)S(1)}, f32[16,1,128]{2,0,1:T(8,128)S(1)}, u32[]{:S(2)}, u32[]{:S(2)}) collective-permute-start(f32[16,1,128]{2,0,1:T(8,128)S(1)} %bitcast.174), channel_id=1, source_target_pairs={{0,64},{64,128},{128,192},{192,256},{256,320},{320,384},{384,448},... | collective-permute-start | bytes 24584 | tf_op jit(solution)/shard_map/ppermute | solution.py:24
  5.6 103.9 %collective-permute-start.1 = (f32[16,1,128]{2,0,1:T(8,128)S(1)}, f32[16,1,128]{2,0,1:T(8,128)S(1)}, u32[]{:S(2)}, u32[]{:S(2)}) collective-permute-start(f32[16,1,128]{2,0,1:T(8,128)S(1)} %bitcast.173), channel_id=1, source_target_pairs={{64,0},{128,64},{192,128},{256,192},{320,256},{384,320},{448,384},... | collective-permute-start | bytes 24584 | tf_op jit(solution)/shard_map/ppermute | solution.py:25
  32.8 81.3 %collective-permute-start.12 = (f32[8,1,64]{2,1,0:T(1,128)S(1)}, f32[8,1,64]{2,1,0:T(1,128)S(1)}, u32[]{:S(2)}, u32[]{:S(2)}) collective-permute-start(f32[8,1,64]{2,1,0:T(1,128)S(1)} %get-tuple-element.87), channel_id=1, source_target_pairs={{0,64},{64,128},{128,192},{192,256},{256,320},{320,384},{384,448},... | collective-permute-start | bytes 6152 | tf_op jit(solution)/shard_map/ppermute | solution.py:24
  39.5 9.9 %collective-permute-start.36 = (f32[2,1,16]{2,1,0:T(1,128)S(1)}, f32[2,1,16]{2,1,0:T(1,128)S(1)}, u32[]{:S(2)}, u32[]{:S(2)}) collective-permute-start(f32[2,1,16]{2,1,0:T(1,128)S(1)} %get-tuple-element.131), channel_id=1, source_target_pairs={{0,64},{64,128},{128,192},{192,256},{256,320},{320,384},{384,448},... | collective-permute-start | bytes 392 | tf_op jit(solution)/shard_map/ppermute | solution.py:24
  49.4 29.1 %collective-permute-start.24 = (f32[4,1,32]{2,1,0:T(1,128)S(1)}, f32[4,1,32]{2,1,0:T(1,128)S(1)}, u32[]{:S(2)}, u32[]{:S(2)}) collective-permute-start(f32[4,1,32]{2,1,0:T(1,128)S(1)} %get-tuple-element.111), channel_id=1, source_target_pairs={{0,64},{64,128},{128,192},{192,256},{256,320},{320,384},{384,448},... | collective-permute-start | bytes 1544 | tf_op jit(solution)/shard_map/ppermute | solution.py:24
  86.3 27.8 %collective-permute-start.13 = (f32[8,1,64]{2,1,0:T(1,128)S(1)}, f32[8,1,64]{2,1,0:T(1,128)S(1)}, u32[]{:S(2)}, u32[]{:S(2)}) collective-permute-start(f32[8,1,64]{2,1,0:T(1,128)S(1)} %get-tuple-element.86), channel_id=1, source_target_pairs={{64,0},{128,64},{192,128},{256,192},{320,256},{384,320},{448,384},... | collective-permute-start | bytes 6152 | tf_op jit(solution)/shard_map/ppermute | solution.py:25
  94.2 167.5 %collective-permute-start.40 = (f32[1,6,18]{2,1,0:T(8,128)}, f32[1,6,18]{2,1,0:T(8,128)}, u32[]{:S(2)}, u32[]{:S(2)}) collective-permute-start(f32[1,6,18]{2,1,0:T(8,128)} %get-tuple-element.121), channel_id=1, source_target_pairs={{0,1},{1,2},{2,3},{3,4},{4,5},{5,6},{6,7},{7,8},{8,9},{9,10},{10,1... | collective-permute-start | bytes 1304 | tf_op jit(solution)/shard_map/ppermute | solution.py:24
  109.7 9.1 %collective-permute-start.2 = (f32[16,34,1]{2,1,0:T(8,128)S(1)}, f32[16,34,1]{2,1,0:T(8,128)S(1)}, u32[]{:S(2)}, u32[]{:S(2)}) collective-permute-start(f32[16,34,1]{2,1,0:T(8,128)S(1)} %get-tuple-element.53), channel_id=1, source_target_pairs={{0,16},{16,32},{32,48},{1,17},{17,33},{33,49},{2,18},{18,34},{34,5... | collective-permute-start | bytes 6536 | tf_op jit(solution)/shard_map/ppermute | solution.py:24
  112.8 10.1 %collective-permute-start.3 = (f32[16,34,1]{2,1,0:T(8,128)S(1)}, f32[16,34,1]{2,1,0:T(8,128)S(1)}, u32[]{:S(2)}, u32[]{:S(2)}) collective-permute-start(f32[16,34,1]{2,1,0:T(8,128)S(1)} %get-tuple-element.52), channel_id=1, source_target_pairs={{16,0},{32,16},{48,32},{17,1},{33,17},{49,33},{18,2},{34,18},{50,3... | collective-permute-start | bytes 6536 | tf_op jit(solution)/shard_map/ppermute | solution.py:25
  128.4 10.0 %collective-permute-start.14 = (f32[8,18,1]{2,0,1:T(8,128)S(1)}, f32[8,18,1]{2,0,1:T(8,128)S(1)}, u32[]{:S(2)}, u32[]{:S(2)}) collective-permute-start(f32[8,18,1]{2,0,1:T(8,128)S(1)} %get-tuple-element.80), channel_id=1, source_target_pairs={{0,16},{16,32},{32,48},{1,17},{17,33},{33,49},{2,18},{18,34},{34,5... | collective-permute-start | bytes 1736 | tf_op jit(solution)/shard_map/ppermute | solution.py:24
  141.7 13.2 %collective-permute-start.8 = (f32[16,34,1]{2,1,0:T(8,128)S(1)}, f32[16,34,1]{2,1,0:T(8,128)S(1)}, u32[]{:S(2)}, u32[]{:S(2)}) collective-permute-start(f32[16,34,1]{2,1,0:T(8,128)S(1)} %get-tuple-element.50), channel_id=1, source_target_pairs={{0,16},{16,32},{32,48},{1,17},{17,33},{33,49},{2,18},{18,34},{34,5... | collective-permute-start | bytes 6536 | tf_op jit(solution)/shard_map/ppermute | solution.py:24
  145.7 10.5 %collective-permute-start.9 = (f32[16,34,1]{2,1,0:T(8,128)S(1)}, f32[16,34,1]{2,1,0:T(8,128)S(1)}, u32[]{:S(2)}, u32[]{:S(2)}) collective-permute-start(f32[16,34,1]{2,1,0:T(8,128)S(1)} %get-tuple-element.51), channel_id=1, source_target_pairs={{16,0},{32,16},{48,32},{17,1},{33,17},{49,33},{18,2},{34,18},{50,3... | collective-permute-start | bytes 6536 | tf_op jit(solution)/shard_map/ppermute | solution.py:25
  147.0 16.8 %collective-permute-start.16 = (f32[1,18,66]{2,0,1:T(1,128)S(1)}, f32[1,18,66]{2,0,1:T(1,128)S(1)}, u32[]{:S(2)}, u32[]{:S(2)}) collective-permute-start(f32[1,18,66]{2,0,1:T(1,128)S(1)} %get-tuple-element.79), channel_id=1, source_target_pairs={{0,1},{1,2},{2,3},{3,4},{4,5},{5,6},{6,7},{7,8},{8,9},{9,10},{10,1... | collective-permute-start | bytes 14264 | tf_op jit(solution)/shard_map/ppermute | solution.py:24
  152.9 14.6 %collective-permute-start.17 = (f32[1,18,66]{2,0,1:T(1,128)S(1)}, f32[1,18,66]{2,0,1:T(1,128)S(1)}, u32[]{:S(2)}, u32[]{:S(2)}) collective-permute-start(f32[1,18,66]{2,0,1:T(1,128)S(1)} %get-tuple-element.78), channel_id=1, source_target_pairs={{1,0},{2,1},{3,2},{4,3},{5,4},{6,5},{7,6},{8,7},{9,8},{10,9},{11,1... | collective-permute-start | bytes 14264 | tf_op jit(solution)/shard_map/ppermute | solution.py:25
  156.3 13.2 %collective-permute-start.10 = (f32[1,34,130]{2,1,0:T(8,128)S(1)}, f32[1,34,130]{2,1,0:T(8,128)S(1)}, u32[]{:S(2)}, u32[]{:S(2)}) collective-permute-start(f32[1,34,130]{2,1,0:T(8,128)S(1)} %get-tuple-element.42), channel_id=1, source_target_pairs={{0,1},{1,2},{2,3},{3,4},{4,5},{5,6},{6,7},{7,8},{8,9},{9,10},{10,1... | collective-permute-start | bytes 53048 | tf_op jit(solution)/shard_map/ppermute | solution.py:24
  163.8 45.9 %collective-permute-start.28 = (f32[1,10,34]{2,0,1:T(1,128)S(1)}, f32[1,10,34]{2,0,1:T(1,128)S(1)}, u32[]{:S(2)}, u32[]{:S(2)}) collective-permute-start(f32[1,10,34]{2,0,1:T(1,128)S(1)} %get-tuple-element.100), channel_id=1, source_target_pairs={{0,1},{1,2},{2,3},{3,4},{4,5},{5,6},{6,7},{7,8},{8,9},{9,10},{10,1... | collective-permute-start | bytes 4088 | tf_op jit(solution)/shard_map/ppermute | solution.py:24
  167.5 44.8 %collective-permute-start.29 = (f32[1,10,34]{2,0,1:T(1,128)S(1)}, f32[1,10,34]{2,0,1:T(1,128)S(1)}, u32[]{:S(2)}, u32[]{:S(2)}) collective-permute-start(f32[1,10,34]{2,0,1:T(1,128)S(1)} %get-tuple-element.101), channel_id=1, source_target_pairs={{1,0},{2,1},{3,2},{4,3},{5,4},{6,5},{7,6},{8,7},{9,8},{10,9},{11,1... | collective-permute-start | bytes 4088 | tf_op jit(solution)/shard_map/ppermute | solution.py:25
  209.8 52.0 %collective-permute-start.41 = (f32[1,6,18]{2,1,0:T(8,128)}, f32[1,6,18]{2,1,0:T(8,128)}, u32[]{:S(2)}, u32[]{:S(2)}) collective-permute-start(f32[1,6,18]{2,1,0:T(8,128)} %get-tuple-element.120), channel_id=1, source_target_pairs={{1,0},{2,1},{3,2},{4,3},{5,4},{6,5},{7,6},{8,7},{9,8},{10,9},{11,1... | collective-permute-start | bytes 1304 | tf_op jit(solution)/shard_map/ppermute | solution.py:25
  212.3 24.8 %collective-permute-start.62 = (f32[1,16,32]{2,1,0:T(8,128)}, f32[1,16,32]{2,1,0:T(8,128)}, u32[]{:S(2)}, u32[]{:S(2)}) collective-permute-start(f32[1,16,32]{2,1,0:T(8,128)} %maximum_select_fusion.17), channel_id=1, source_target_pairs={{0,1},{1,0},{2,3},{3,2},{4,5},{5,4},{6,7},{7,6},{8,9},{9,8},{10,11... | collective-permute-start | bytes 6152 | tf_op jit(solution)/shard_map/ppermute | solution.py:14
  230.8 11.2 %collective-permute-start.30 = (f32[4,1,32]{2,1,0:T(1,128)S(1)}, f32[4,1,32]{2,1,0:T(1,128)S(1)}, u32[]{:S(2)}, u32[]{:S(2)}) collective-permute-start(f32[4,1,32]{2,1,0:T(1,128)S(1)} %get-tuple-element.108), channel_id=1, source_target_pairs={{0,64},{64,128},{128,192},{192,256},{256,320},{320,384},{384,448},... | collective-permute-start | bytes 1544 | tf_op jit(solution)/shard_map/ppermute | solution.py:24
  237.9 9.7 %collective-permute-start.63 = (f32[2,16,32]{2,1,0:T(8,128)S(1)}, f32[2,16,32]{2,1,0:T(8,128)S(1)}, u32[]{:S(2)}, u32[]{:S(2)}) collective-permute-start(f32[2,16,32]{2,1,0:T(8,128)S(1)} %maximum_select_fusion.7), channel_id=1, source_target_pairs={{0,2},{1,3},{2,0},{3,1},{4,6},{5,7},{6,4},{7,5},{8,10},{9,11},{10,... | collective-permute-start | bytes 12296 | tf_op jit(solution)/shard_map/ppermute | solution.py:14
  262.9 15.7 %collective-permute-start.42 = (f32[2,1,16]{2,1,0:T(1,128)S(1)}, f32[2,1,16]{2,1,0:T(1,128)S(1)}, u32[]{:S(2)}, u32[]{:S(2)}) collective-permute-start(f32[2,1,16]{2,1,0:T(1,128)S(1)} %get-tuple-element.126), channel_id=1, source_target_pairs={{0,64},{64,128},{128,192},{192,256},{256,320},{320,384},{384,448},... | collective-permute-start | bytes 392 | tf_op jit(solution)/shard_map/ppermute | solution.py:24
  266.4 12.2 %collective-permute-start.43 = (f32[2,1,16]{2,1,0:T(1,128)S(1)}, f32[2,1,16]{2,1,0:T(1,128)S(1)}, u32[]{:S(2)}, u32[]{:S(2)}) collective-permute-start(f32[2,1,16]{2,1,0:T(1,128)S(1)} %get-tuple-element.127), channel_id=1, source_target_pairs={{64,0},{128,64},{192,128},{256,192},{320,256},{384,320},{448,384},... | collective-permute-start | bytes 392 | tf_op jit(solution)/shard_map/ppermute | solution.py:25
  267.7 25.0 %collective-permute-start.64 = (f32[4,16,32]{2,1,0:T(8,128)S(1)}, f32[4,16,32]{2,1,0:T(8,128)S(1)}, u32[]{:S(2)}, u32[]{:S(2)}) collective-permute-start(f32[4,16,32]{2,1,0:T(8,128)S(1)} %maximum_select_fusion.5), channel_id=1, source_target_pairs={{0,4},{1,5},{2,6},{3,7},{4,0},{5,1},{6,2},{7,3},{8,12},{9,13},{10,... | collective-permute-start | bytes 24584 | tf_op jit(solution)/shard_map/ppermute | solution.py:14
  296.8 9.9 %collective-permute-start.48 = (f32[1,2,8]{2,1,0:T(2,128)S(1)}, f32[1,2,8]{2,1,0:T(2,128)S(1)}, u32[]{:S(2)}, u32[]{:S(2)}) collective-permute-start(f32[1,2,8]{2,1,0:T(2,128)S(1)} %get-tuple-element.132), channel_id=1, source_target_pairs={{0,64},{64,0},{128,192},{192,128},{256,320},{320,256},{384,448},{4... | collective-permute-start | bytes 200 | tf_op jit(solution)/shard_map/ppermute | solution.py:14
  301.1 39.7 %collective-permute-start.65 = (f32[8,16,32]{2,1,0:T(8,128)S(1)}, f32[8,16,32]{2,1,0:T(8,128)S(1)}, u32[]{:S(2)}, u32[]{:S(2)}) collective-permute-start(f32[8,16,32]{2,1,0:T(8,128)S(1)} %maximum_select_fusion.3), channel_id=1, source_target_pairs={{0,8},{1,9},{2,10},{3,11},{4,12},{5,13},{6,14},{7,15},{8,0},{9,1},... | collective-permute-start | bytes 49160 | tf_op jit(solution)/shard_map/ppermute | solution.py:14
  354.6 9.0 %collective-permute-start.56 = (f32[8,16,32]{2,1,0:T(8,128)S(1)}, f32[8,16,32]{2,1,0:T(8,128)S(1)}, u32[]{:S(2)}, u32[]{:S(2)}) collective-permute-start(f32[8,16,32]{2,1,0:T(8,128)S(1)} %maximum_select_fusion.2), channel_id=1, source_target_pairs={{0,8},{1,9},{2,10},{3,11},{4,12},{5,13},{6,14},{7,15},{8,0},{9,1},... | collective-permute-start | bytes 49160 | tf_op jit(solution)/shard_map/ppermute | solution.py:14
  391.9 11.2 %collective-permute-start.70 = (f32[1,6,18]{2,1,0:T(8,128)S(1)}, f32[1,6,18]{2,1,0:T(8,128)S(1)}, u32[]{:S(2)}, u32[]{:S(2)}) collective-permute-start(f32[1,6,18]{2,1,0:T(8,128)S(1)} %get-tuple-element.112), channel_id=1, source_target_pairs={{0,1},{1,2},{2,3},{3,4},{4,5},{5,6},{6,7},{7,8},{8,9},{9,10},{10,1... | collective-permute-start | bytes 1304 | tf_op jit(solution)/shard_map/ppermute | solution.py:24
  463.6 9.2 %collective-permute-start.86 = (f32[16,34,1]{2,1,0:T(8,128)S(1)}, f32[16,34,1]{2,1,0:T(8,128)S(1)}, u32[]{:S(2)}, u32[]{:S(2)}) collective-permute-start(f32[16,34,1]{2,1,0:T(8,128)S(1)} %get-tuple-element.48), channel_id=1, source_target_pairs={{0,16},{16,32},{32,48},{1,17},{17,33},{33,49},{2,18},{18,34},{34,5... | collective-permute-start | bytes 6536 | tf_op jit(solution)/shard_map/ppermute | solution.py:24
  465.2 11.4 %collective-permute-start.87 = (f32[16,34,1]{2,1,0:T(8,128)S(1)}, f32[16,34,1]{2,1,0:T(8,128)S(1)}, u32[]{:S(2)}, u32[]{:S(2)}) collective-permute-start(f32[16,34,1]{2,1,0:T(8,128)S(1)} %get-tuple-element.49), channel_id=1, source_target_pairs={{16,0},{32,16},{48,32},{17,1},{33,17},{49,33},{18,2},{34,18},{50,3... | collective-permute-start | bytes 6536 | tf_op jit(solution)/shard_map/ppermute | solution.py:25
  494.6 9.1 %collective-permute-start.92 = (f32[16,34,1]{2,1,0:T(8,128)S(1)}, f32[16,34,1]{2,1,0:T(8,128)S(1)}, u32[]{:S(2)}, u32[]{:S(2)}) collective-permute-start(f32[16,34,1]{2,1,0:T(8,128)S(1)} %get-tuple-element.46), channel_id=1, source_target_pairs={{0,16},{16,32},{32,48},{1,17},{17,33},{33,49},{2,18},{18,34},{34,5... | collective-permute-start | bytes 6536 | tf_op jit(solution)/shard_map/ppermute | solution.py:24
  496.5 11.6 %collective-permute-start.93 = (f32[16,34,1]{2,1,0:T(8,128)S(1)}, f32[16,34,1]{2,1,0:T(8,128)S(1)}, u32[]{:S(2)}, u32[]{:S(2)}) collective-permute-start(f32[16,34,1]{2,1,0:T(8,128)S(1)} %get-tuple-element.47), channel_id=1, source_target_pairs={{16,0},{32,16},{48,32},{17,1},{33,17},{49,33},{18,2},{34,18},{50,3... | collective-permute-start | bytes 6536 | tf_op jit(solution)/shard_map/ppermute | solution.py:25
  (150 other events, 3625.7 us)
where the time goes:
time: 522 us; the launch traced here: 518 us
  starting transfers between devices  288 us (55%)
  waiting for transfers between devices  128 us (25%)
  local copies, waits for them, and re-layouts  55.2 us (11%)
  other arithmetic  44 us (8%)
    ppermute x39, starting transfers between devices, padded(): before = lax.ppermute(last, axis, up)  152 us
    ppermute x39, waiting for transfers between devices, padded(): after = lax.ppermute(first, axis, down)  85.3 us
    ppermute x18, starting transfers between devices, from_partner(): lax.ppermute(x, axis, [(i, i ^ 1 << distance) for i in range(lax.axis_siz...  76.6 us
    ppermute x39, starting transfers between devices, padded(): after = lax.ppermute(first, axis, down)  58.9 us
    reshape x6, local copies, waits for them, and re-layouts, restrict(): block.reshape(layers // 2, 2, rows_count // 2, 2, columns // 2, 2)  42.4 us
    ppermute x18, waiting for transfers between devices, from_partner(): lax.ppermute(x, axis, [(i, i ^ 1 << distance) for i in range(lax.axis_siz...  24.1 us
    ppermute x39, waiting for transfers between devices, padded(): before = lax.ppermute(last, axis, up)  18.3 us
    reduce_sum x14, other arithmetic, restrict(): block.reshape(layers // 2, 2, rows_count // 2, 2, columns // 2, 2)  18.3 us
  transfers between devices with their start and end apart: 96, of which 44 were waited for; matrix products, arithmetic and copies ran while one was open for 15% of the time, Pallas kernels for 0%

commit v1 on v0

v1 whole, which is shorter than its diff:
```python
import jax
import jax.numpy as jnp
from jax import lax
from jax.experimental import pallas as pl
from jax.experimental.pallas import tpu as pltpu
from jax.sharding import PartitionSpec as P

MESH = pl.DeviceIdType.MESH
AXES = ("gx", "gy", "gz")
OMEGA = 2.0 / 3.0
LANES = 128
F32 = jnp.float32

FINE = ((16, 32), (8, 16), (4, 8), (2, 4))
COARSE = ((16, 16, 4), (8, 8, 8), (4, 4, 16))
SWAP_FIELDS = ("w0", "w1", "w2", "w3", "v0", "v1", "v2", "v3", "c3", "c2", "c1", "c0", "r0")


def padded_rows(rows):
    return max(rows, 8)


def lane_of(shape):
    return lax.broadcasted_iota(jnp.int32, shape, len(shape) - 1)


def row_of(shape):
    return lax.broadcasted_iota(jnp.int32, shape, len(shape) - 2)


def loop(count, body, carry):
    if count <= 4:
        for i in range(count):
            carry = body(i, carry)
        return carry
    return lax.fori_loop(0, count, body, carry, unroll=2)


def shift_lanes(x, amount):
    amount = lax.rem(amount + LANES, LANES) if not isinstance(amount, int) else amount % LANES
    if isinstance(amount, int) and amount == 0:
        return x
    return pltpu.roll(x, amount, 1)


def one_hot(cond):
    return jnp.where(cond, 1.0, 0.0).astype(F32)


def exact_dot(a, b):
    return jnp.dot(a, b, precision=lax.Precision.HIGHEST, preferred_element_type=F32)


class Swap:
    def __init__(self, refs, sems, level, place):
        self.ext, self.yf, self.yl, self.yhi, self.ylo, self.px, self.xlo, self.xhi, self.side = refs
        self.send, self.recv = sems
        self.planes, self.rows = FINE[level]
        self.half = 2**level
        self.place = place
        self.copies = []

    def put(self, z, x, packed):
        self.ext[z + 1] = x
        self.yf[z] = x[0:1]
        self.yl[z] = x[self.rows - 1 : self.rows]
        moved = shift_lanes(x, 2 * self.half * z + self.half)
        return jnp.where(lane_of(x.shape) // (2 * self.half) == z, moved, packed)

    def empty(self):
        return jnp.zeros(self.px.shape, F32)

    def start(self, packed):
        self.px[...] = packed
        n = self.planes
        at, size = self.place
        moves = (
            ("gz", 1, self.ext.at[n], self.ext.at[0]),
            ("gz", -1, self.ext.at[1], self.ext.at[n + 1]),
            ("gx", 1, self.yl, self.ylo),
            ("gx", -1, self.yf, self.yhi),
            ("gy", 1, self.px, self.xlo),
            ("gy", -1, self.px, self.xhi),
        )
        for i, (axis, step, src, dst) in enumerate(moves):
            to = tuple(
                lax.rem(at[a] + step + size[a], size[a]) if a == axis else at[a] for a in AXES
            )
            copy = pltpu.make_async_remote_copy(
                src_ref=src,
                dst_ref=dst,
                send_sem=self.send.at[i],
                recv_sem=self.recv.at[i],
                device_id=to,
                device_id_type=MESH,
            )
            copy.start()
            self.copies.append(copy)

    def finish(self):
        at, size = self.place
        for copy in self.copies:
            copy.wait()
        n = self.planes
        self.ext[0] = jnp.where(at["gz"] > 0, self.ext[0], 0.0)
        self.ext[n + 1] = jnp.where(at["gz"] < size["gz"] - 1, self.ext[n + 1], 0.0)
        self.ylo[...] = jnp.where(at["gx"] > 0, self.ylo[...], 0.0)
        self.yhi[...] = jnp.where(at["gx"] < size["gx"] - 1, self.yhi[...], 0.0)
        low = jnp.where(at["gy"] > 0, self.xlo[...], 0.0)
        high = jnp.where(at["gy"] < size["gy"] - 1, self.xhi[...], 0.0)
        self.side[...] = jnp.where(lane_of(low.shape) % (2 * self.half) < self.half, low, high)

    def around(self, z):
        x = self.ext[z + 1]
        row, lane = row_of(x.shape), lane_of(x.shape)
        tall, half = x.shape[0], self.half
        side = shift_lanes(self.side[...], -(2 * half * z + half))
        return x, (
            self.ext[z],
            self.ext[z + 2],
            jnp.where(row == 0, self.ylo[z], pltpu.roll(x, 1, 0)),
            jnp.where(row == self.rows - 1, self.yhi[z], pltpu.roll(x, tall - 1, 0)),
            shift_lanes(jnp.where(lane >= LANES - half, side, x), half),
            shift_lanes(jnp.where(lane < half, side, x), -half),
        )


class Whole:
    def __init__(self, ext, shape):
        self.ext = ext
        self.planes, self.rows, self.half = shape
        self.ext[0] = jnp.zeros(self.ext.shape[1:], F32)
        self.ext[self.planes + 1] = jnp.zeros(self.ext.shape[1:], F32)

    def put(self, z, x, packed):
        self.ext[z + 1] = x
        return packed

    def around(self, z):
        return beside(self.ext[z], self.ext[z + 1], self.ext[z + 2], self.rows, self.half)


def beside(before, x, after, rows, half):
    row, lane = row_of(x.shape), lane_of(x.shape)
    return x, (
        before,
        after,
        jnp.where(row == 0, 0.0, pltpu.roll(x, 1, 0)),
        jnp.where(row == rows - 1, 0.0, pltpu.roll(x, x.shape[0] - 1, 0)),
        shift_lanes(jnp.where(lane >= LANES - half, 0.0, x), half),
        shift_lanes(jnp.where(lane < half, 0.0, x), -half),
    )


def applied(around, faces, z):
    x, near = around
    total = faces[0, z] * (x - near[0])
    for q in range(1, 6):
        total = total + faces[q, z] * (x - near[q])
    return total


def face_weights(field, faces, rate, level):
    scale = 0.5 * 0.25**level

    def body(z, carry):
        x, near = field.around(z)
        diagonal = jnp.zeros_like(x)
        for q in range(6):
            weight = scale * (x + near[q])
            faces[q, z] = weight
            diagonal = diagonal + weight
        inside = diagonal > 0.0
        rate[z] = jnp.where(inside, OMEGA / jnp.where(inside, diagonal, 1.0), 0.0)
        return carry

    loop(field.planes, body, 0)


def pair_down(total, rows, half, scratch):
    scratch[...] = total
    count = total.shape[0] // 2
    both = scratch[pl.ds(0, count, stride=2), :] + scratch[pl.ds(1, count, stride=2), :]
    lane = lane_of(both.shape)
    other = jnp.where(lane // half % 2 == 0, shift_lanes(both, -half), shift_lanes(both, half))
    return 0.125 * (both + other)


def spread(coarse, rows, scratch):
    count = scratch.shape[0] // 2
    scratch[pl.ds(0, count, stride=2), :] = coarse[0:count]
    scratch[pl.ds(1, count, stride=2), :] = coarse[0:count]
    return scratch[...]


def store_layer(dst, z, layer):
    dst[z, 0 : layer.shape[0]] = layer


def down(field, source, faces, level_half, target, scratch):
    def body(z, carry):
        total = None
        for part in range(2):
            i = 2 * z + part
            defect = source[i] - applied(field.around(i), faces, i)
            total = defect if total is None else total + defect
        store_layer(target, z, pair_down(total, field.rows, level_half, scratch))
        return carry

    loop(field.planes // 2, body, 0)


def first_relax(field, source, rate, packed):
    def body(z, carry):
        return field.put(z, rate[z] * source[z], carry)

    return loop(field.planes, body, packed)


def add_coarse(field, old, coarse_layer, packed, scratch):
    def body(z, carry):
        wide = spread(coarse_layer(z), field.rows, scratch)
        for part in range(2):
            i = 2 * z + part
            carry = field.put(i, old.ext[i + 1] + wide, carry)
        return carry

    return loop(field.planes // 2, body, packed)


def relax_into(field, source, faces, rate, put, carry):
    def body(z, carry):
        around = field.around(z)
        return put(z, around[0] + rate[z] * (source[z] - applied(around, faces, z)), carry)

    return loop(field.planes, body, carry)


def restrict_weights(layer, planes, rows, half, target, scratch):
    def body(z, carry):
        store_layer(target, z, pair_down(layer(2 * z) + layer(2 * z + 1), rows, half, scratch))
        return carry

    loop(planes // 2, body, 0)


def kernel(size, names, source_ref, weight_ref, out_ref, residual_ref, *scratch):
    ref = dict(zip(names, scratch))
    at = {a: lax.axis_index(a) for a in AXES}
    place = (at, size)

    def along(axis, step):
        return tuple(lax.rem(at[a] + step, size[a]) if a == axis else at[a] for a in AXES)

    barrier = pltpu.get_barrier_semaphore()
    peers = [(a, k) for a in AXES for k in range(1, size[a])]
    for axis, step in peers:
        pl.semaphore_signal(barrier, inc=1, device_id=along(axis, step), device_id_type=MESH)

    swaps = {}
    for k, name in enumerate(SWAP_FIELDS):
        parts = ("ext", "yf", "yl", "yhi", "ylo", "px", "xlo", "xhi", "side")
        swaps[name] = Swap(
            tuple(ref[f"{name}_{part}"] for part in parts),
            (ref["send"].at[k], ref["recv"].at[k]),
            int(name[1]),
            place,
        )

    for level in range(4):
        planes, rows = FINE[level]
        if level > 0:
            ref[f"s{level}"][...] = jnp.zeros(ref[f"s{level}"].shape, F32)
            ref[f"k{level}"][...] = jnp.zeros(ref[f"k{level}"].shape, F32)
            below = weight_ref if level == 1 else ref[f"k{level - 1}"]
            restrict_weights(
                lambda z, below=below: below[z],
                2 * planes,
                2 * rows,
                2 ** (level - 1),
                ref[f"k{level}"],
                ref[f"t{level - 1}"],
            )
    ref["s4"][...] = jnp.zeros(ref["s4"].shape, F32)
    ref["k4"][...] = jnp.zeros(ref["k4"].shape, F32)
    restrict_weights(lambda z: ref["k3"][z], 2, 4, 8, ref["k4"], ref["t3"])
    packed = {}
    for level in range(4):
        swap = swaps[f"w{level}"]
        below = weight_ref if level == 0 else ref[f"k{level}"]
        packed[level] = loop(
            swap.planes,
            lambda z, c, swap=swap, below=below: swap.put(z, below[z], c),
            swap.empty(),
        )
    pl.semaphore_wait(barrier, len(peers))
    for level in range(4):
        swaps[f"w{level}"].start(packed[level])
    for level in range(4):
        swap = swaps[f"w{level}"]
        swap.finish()
        face_weights(swap, ref[f"f{level}"], ref[f"d{level}"], level)

    sources = [source_ref, ref["s1"], ref["s2"], ref["s3"], ref["s4"]]
    for level in range(4):
        swap = swaps[f"v{level}"]
        swap.start(first_relax(swap, sources[level], ref[f"d{level}"], swap.empty()))
        swap.finish()
        down(swap, sources[level], ref[f"f{level}"], 2**level, sources[level + 1], ref[f"t{level}"])

    tile = (8, LANES)
    lane, row = lane_of(tile), row_of(tile)
    own = jnp.concatenate([ref["s4"][0][0:2], ref["k4"][0][0:2], jnp.zeros((4, LANES), F32)], 0)
    square = (LANES, LANES)
    pick = one_hot(row_of(square) == lane_of(square) % 8 * 16)
    shrunk = exact_dot(own, pick)
    line = jnp.sum(jnp.where(lane // 32 == row, shrunk, 0.0), axis=0, keepdims=True)
    ref["g0"][...] = line

    def all_to_all(axis, src, dst, send, recv):
        copies = []
        for step in range(1, size[axis]):
            copy = pltpu.make_async_remote_copy(
                src_ref=src,
                dst_ref=dst.at[at[axis]],
                send_sem=send.at[step],
                recv_sem=recv.at[step],
                device_id=along(axis, step),
                device_id_type=MESH,
            )
            copy.start()
            copies.append(copy)
        dst[at[axis]] = src[...]
        for copy in copies:
            copy.wait()

    all_to_all("gy", ref["g0"], ref["g1"], ref["send_gy"], ref["recv_gy"])
    lane1 = lane_of((1, LANES))
    merged = jnp.zeros((1, LANES), F32)
    for k in range(size["gy"]):
        merged = jnp.where(lane1 // 8 % 4 == k, ref["g1"][k], merged)
    ref["g2"][...] = merged
    all_to_all("gz", ref["g2"], ref["g3"], ref["send_gz"], ref["recv_gz"])
    all_to_all("gx", ref["g3"], ref["g4"], ref["send_gx"], ref["recv_gx"])

    wide = (LANES, 4 * LANES)
    expand = one_hot(row_of(wide) == lane_of(wide) // LANES * 32 + lane_of(wide) % LANES // 4)
    for z in range(size["gz"]):
        for k in range(size["gx"]):
            ref["g5"][8 * z + k : 8 * z + k + 1, :] = ref["g4"][k, z]
    ref["g6"][...] = exact_dot(ref["g5"][...], expand)
    fields = {}
    for level in range(4, 7):
        for kind in "wvc":
            fields[kind, level] = Whole(ref[f"{kind}{level}_ext"], COARSE[level - 4])
    for z in range(16):
        block = ref["g6"][8 * z : 8 * z + 8, :]
        for part in range(2):
            rows = pl.ds(part, 8, stride=2)
            ref["q4"][z, rows, :] = block[:, part * LANES : (part + 1) * LANES]
            ref["w4_ext"][z + 1, rows, :] = block[:, (part + 2) * LANES : (part + 3) * LANES]

    for level in (4, 5):
        planes, rows, half = COARSE[level - 4]
        field = fields["w", level]
        if level == 5:
            ref["k6"][...] = jnp.zeros(ref["k6"].shape, F32)
            ref["q6"][...] = jnp.zeros(ref["q6"].shape, F32)
        target = ref[f"k{level + 1}"]
        restrict_weights(
            lambda z, field=field: field.ext[z + 1], planes, rows, half, target, ref[f"t{level}"]
        )
        for z in range(planes // 2):
            fields["w", level + 1].put(z, target[z], 0)
    for level in (4, 5, 6):
        face_weights(fields["w", level], ref[f"f{level}"], ref[f"d{level}"], level)
    for level in (4, 5):
        field, faces = fields["v", level], ref[f"f{level}"]
        first_relax(field, ref[f"q{level}"], ref[f"d{level}"], 0)
        down(field, ref[f"q{level}"], faces, field.half, ref[f"q{level + 1}"], ref[f"t{level}"])

    planes, rows, half = COARSE[2]
    faces, rate, source = ref["f6"], ref["d6"], ref["q6"]
    zero = jnp.zeros((8, LANES), F32)

    def sweep(_, value):
        out = []
        for z in range(planes):
            before = value[z - 1] if z > 0 else zero
            after = value[z + 1] if z < planes - 1 else zero
            around = beside(before, value[z], after, rows, half)
            out.append(value[z] + rate[z] * (source[z] - applied(around, faces, z)))
        return tuple(out)

    start = tuple(rate[z] * source[z] for z in range(planes))
    bottom = lax.fori_loop(0, 7, sweep, start)
    for z in range(planes):
        ref["e6"][z] = bottom[z]
    for level in (5, 4):
        field = fields["c", level]
        coarse = ref[f"e{level + 1}"]
        add_coarse(
            field, fields["v", level], lambda z, c=coarse: c[z], 0, ref[f"t{level}"]
        )
        target = ref[f"e{level}"]

        def put(z, x, carry, target=target):
            target[z] = x
            return carry

        relax_into(field, ref[f"q{level}"], ref[f"f{level}"], ref[f"d{level}"], put, 0)

    pick_lane = one_hot(row_of(square) == (8 * at["gy"] + lane_of(square) // 16) * 4)
    pick_row = one_hot(lane_of((8, 16)) == 2 * at["gx"] + row_of((8, 16)))
    mine = exact_dot(pick_row, exact_dot(ref["e4"][at["gz"]], pick_lane))
    ref["e_own"][...] = mine

    coarse_layer = lambda z: ref["e_own"][...]
    for level in (3, 2, 1, 0):
        swap = swaps[f"c{level}"]
        old = swaps[f"v{level}"]
        swap.start(add_coarse(swap, old, coarse_layer, swap.empty(), ref[f"t{level}"]))
        swap.finish()
        source, faces, rate = sources[level], ref[f"f{level}"], ref[f"d{level}"]
        if level > 0:
            target = ref[f"e{level}"]

            def put(z, x, carry, target=target):
                target[z] = x
                return carry

            relax_into(swap, source, faces, rate, put, 0)
            coarse_layer = lambda z, target=target: target[z]
        else:
            last = swaps["r0"]

            def put(z, x, carry):
                out_ref[z] = x
                return last.put(z, x, carry)

            last.start(relax_into(swap, source, faces, rate, put, last.empty()))
            last.finish()

            def body(z, carry):
                residual_ref[z] = source[z] - applied(last.around(z), faces, z)
                return carry

            loop(16, body, 0)


def buffers(size):
    shapes = {}

    def vmem(name, *shape):
        shapes[name] = pltpu.VMEM(shape, F32)

    for name in SWAP_FIELDS:
        planes, rows = FINE[int(name[1])]
        tall = padded_rows(rows)
        vmem(f"{name}_ext", planes + 2, tall, LANES)
        for part in ("yf", "yl", "yhi", "ylo"):
            vmem(f"{name}_{part}", planes, 1, LANES)
        for part in ("px", "xlo", "xhi", "side"):
            vmem(f"{name}_{part}", tall, LANES)
    for level, (planes, rows) in enumerate(FINE):
        tall = padded_rows(rows)
        vmem(f"f{level}", 6, planes, tall, LANES)
        vmem(f"d{level}", planes, tall, LANES)
        vmem(f"t{level}", tall, LANES)
        if level > 0:
            vmem(f"s{level}", planes, tall, LANES)
            vmem(f"k{level}", planes, tall, LANES)
            vmem(f"e{level}", planes, tall, LANES)
    vmem("s4", 1, 8, LANES)
    vmem("k4", 1, 8, LANES)
    vmem("e_own", 8, LANES)
    for level, (planes, rows, _) in zip((4, 5, 6), COARSE):
        tall = padded_rows(rows)
        for kind in "wvc":
            vmem(f"{kind}{level}_ext", planes + 2, tall, LANES)
        vmem(f"f{level}", 6, planes, tall, LANES)
        vmem(f"d{level}", planes, tall, LANES)
        vmem(f"q{level}", planes, tall, LANES)
        vmem(f"e{level}", planes, tall, LANES)
        vmem(f"t{level}", tall, LANES)
        if level > 4:
            vmem(f"k{level}", planes, tall, LANES)
    vmem("g0", 1, LANES)
    vmem("g1", size["gy"], 1, LANES)
    vmem("g2", 1, LANES)
    vmem("g3", size["gz"], 1, LANES)
    vmem("g4", size["gx"], size["gz"], 1, LANES)
    vmem("g5", size["gx"] * size["gz"], LANES)
    vmem("g6", size["gx"] * size["gz"], 4 * LANES)
    shapes["send"] = pltpu.SemaphoreType.DMA((len(SWAP_FIELDS), 6))
    shapes["recv"] = pltpu.SemaphoreType.DMA((len(SWAP_FIELDS), 6))
    for axis in AXES:
        shapes[f"send_{axis}"] = pltpu.SemaphoreType.DMA((size[axis],))
        shapes[f"recv_{axis}"] = pltpu.SemaphoreType.DMA((size[axis],))
    return shapes


def solution(mesh):
    size = dict(mesh.shape)
    spec = P("gz", "gx", "gy")

    def body(source, conductivity):
        shapes = buffers(size)
        block = jax.ShapeDtypeStruct(source.shape, F32)

        def run(*refs):
            kernel(size, tuple(shapes), *refs)

        return pl.pallas_call(
            run,
            out_shape=(block, block),
            in_specs=[pl.BlockSpec(memory_space=pltpu.VMEM)] * 2,
            out_specs=[pl.BlockSpec(memory_space=pltpu.VMEM)] * 2,
            scratch_shapes=list(shapes.values()),
            compiler_params=pltpu.CompilerParams(
                collective_id=0, has_side_effects=True, vmem_limit_bytes=48 * 1024 * 1024
            ),
        )(source, conductivity)

    return jax.shard_map(
        body, mesh=mesh, in_specs=(spec, spec), out_specs=(spec, spec), check_vma=False
    )
```

time: 522 us -> 81.6 us (0.16)
  starting transfers between devices: 288 us -> 0 us
  waiting for transfers between devices: 128 us -> 0 us
  Pallas kernels: 0 us -> 77.5 us
  local copies, waits for them, and re-layouts: 55.2 us -> 3.3 us
  other arithmetic: 44 us -> 0 us
    ppermute x96 -> x0, starting transfers between devices: 288 us -> none  [the longest x39 152 us: padded(): before = lax.ppermute(last, axis, up)]
    ppermute x96 -> x0, waiting for transfers between devices: 128 us -> none  [the longest x39 85.3 us: padded(): after = lax.ppermute(first, axis, down)]
    pallas_call x0 -> x1, Pallas kernels: none -> 77.5 us  [body(): pl.pallas_call(run, out_shape=(block, block), in_specs=[pl.BlockSpec(memo...]
    reshape x16 -> x0, local copies, waits for them, and re-layouts: 43.9 us -> none  [the longest x6 42.4 us: restrict(): block.reshape(layers // 2, 2, rows_count // 2, 2, columns // 2, 2)]
    reduce_sum x14 -> x0, other arithmetic: 18.3 us -> none  [restrict(): block.reshape(layers // 2, 2, rows_count // 2, 2, columns // 2, 2)]
    div x7 -> x0, other arithmetic: 7.32 us -> none  [the longest x4 3.74 us: relax_faces(): return crop(field, 1) + OMEGA * (source - applied) / safe]
    sub x6 -> x0, other arithmetic: 5.76 us -> none  [the longest x3 2.4 us: body(): sources.append(restrict(sources[level] - applied))]
  transfers between devices with their start and end apart: 96 -> 0, of which waited for: 44 -> 0; matrix products, arithmetic and copies ran while one was open for 15% -> 0% of each run, Pallas kernels for 0% -> 0%
where the time goes in v1:
time: 81.6 us; the launch traced here: 81.5 us
  Pallas kernels  77.5 us (95%)
  local copies, waits for them, and re-layouts  3.3 us (4%)
    pallas_call x1, Pallas kernels, body(): pl.pallas_call(run, out_shape=(block, block), in_specs=[pl.BlockSpec(memo...  77.5 us
    unnamed x6, local copies, waits for them, and re-layouts  3.3 us

profile of v1, /device:TPU:1, one launch (start us, length us, event | category | flops | bytes accessed | tf_op | source)
XLA Modules:
  0.0 81.5 jit_solution(121747682575883440)
XLA Ops:
  0.6 0.0 copy-start
  0.6 0.9 %copy-done = f32[16,32,128]{2,1,0:T(8,128)S(1)} copy-done((f32[16,32,128]{2,1,0:T(8,128)S(1)}, f32[16,32,128]{2,1,0:T(8,128)}, u32[]{:S(2)}) %copy-start) | copy-done | bytes 262168
  1.6 0.0 copy-start.1
  1.6 0.9 %copy-done.1 = f32[16,32,128]{2,1,0:T(8,128)S(1)} copy-done((f32[16,32,128]{2,1,0:T(8,128)S(1)}, f32[16,32,128]{2,1,0:T(8,128)}, u32[]{:S(2)}) %copy-start.1) | copy-done | bytes 262168
  2.5 77.5 %shard_map.41 = (f32[16,32,128]{2,1,0:T(8,128)S(1)}, f32[16,32,128]{2,1,0:T(8,128)S(1)}) custom-call(f32[16,32,128]{2,1,0:T(8,128)S(1)} %copy-done, f32[16,32,128]{2,1,0:T(8,128)S(1)} %copy-done.1), custom_call_target="tpu_custom_call" | custom-call | tf_op jit(solution)/shard_map/pallas_call | solution.py:514
  80.1 0.7 copy.6
  80.8 0.7 copy.7
Async XLA Ops:
  0.6 1.0 %copy-start = (f32[16,32,128]{2,1,0:T(8,128)S(1)}, f32[16,32,128]{2,1,0:T(8,128)}, u32[]{:S(2)}) copy-start(f32[16,32,128]{2,1,0:T(8,128)} %refs_0_.1) | copy-start | bytes 786436
  1.6 0.9 %copy-start.1 = (f32[16,32,128]{2,1,0:T(8,128)S(1)}, f32[16,32,128]{2,1,0:T(8,128)}, u32[]{:S(2)}) copy-start(f32[16,32,128]{2,1,0:T(8,128)} %refs_1_.1) | copy-start | bytes 786436

commit v2 on v1

--- a/solution.py
+++ b/solution.py
@@ -11,9 +11,12 @@
 LANES = 128
 F32 = jnp.float32
 
-FINE = ((16, 32), (8, 16), (4, 8), (2, 4))
+FINE = ((16, 32),)
+RING = {1: (24, 32, 1), 2: (12, 16, 2), 3: (6, 8, 4)}
+MARGIN = 8
 COARSE = ((16, 16, 4), (8, 8, 8), (4, 4, 16))
-SWAP_FIELDS = ("w0", "w1", "w2", "w3", "v0", "v1", "v2", "v3", "c3", "c2", "c1", "c0", "r0")
+SWAP_FIELDS = ("w0", "v0", "c0", "r0")
+SIDES = tuple((a, b, c) for a in (-1, 0, 1) for b in (-1, 0, 1) for c in (-1, 0, 1) if (a, b, c) != (0, 0, 0))
 
 
 def padded_rows(rows):
@@ -125,6 +128,118 @@
         )
 
 
+class Ring:
+    def __init__(self, ext, level):
+        self.ext = ext
+        self.planes, self.rows, self.half = RING[level]
+
+    def put(self, z, x, carry):
+        self.ext[z] = x
+        return carry
+
+    def around(self, z):
+        n = self.planes
+        if isinstance(z, int):
+            before, after = (z + n - 1) % n, (z + 1) % n
+        else:
+            before, after = lax.rem(z + n - 1, n), lax.rem(z + 1, n)
+        x = self.ext[z]
+        return x, (
+            self.ext[before],
+            self.ext[after],
+            pltpu.roll(x, 1, 0),
+            pltpu.roll(x, x.shape[0] - 1, 0),
+            shift_lanes(x, self.half),
+            shift_lanes(x, -self.half),
+        )
+
+
+def ring_loop(first, count, total, body):
+    def step(i, carry):
+        z = first + i
+        body(z % total if isinstance(z, int) else lax.rem(z, total))
+        return carry
+
+    loop(count, step, 0)
+
+
+class Margin:
+    def __init__(self, ext, px, left, right, sems, place):
+        self.ext, self.px, self.left, self.right = ext, px, left, right
+        self.send, self.recv = sems
+        self.place = place
+        self.copies = []
+
+    def start(self):
+        lane = lane_of((16, LANES))
+        packed = jnp.zeros((16, LANES), F32)
+        for z in range(MARGIN):
+            x = self.ext[z, 0:16]
+            spot = lane // 16 == z
+            packed = jnp.where(spot & (lane % 16 < 8), shift_lanes(x, 16 * z - 64), packed)
+            packed = jnp.where(spot & (lane % 16 >= 8), shift_lanes(x, 16 * z), packed)
+        self.px[...] = packed
+        at, size = self.place
+        rows_out = {-1: pl.ds(0, 8), 0: pl.ds(0, 16), 1: pl.ds(8, 8)}
+        rows_in = {-1: pl.ds(16, 8), 0: pl.ds(0, 16), 1: pl.ds(24, 8)}
+        planes_in = {-1: pl.ds(8, 8), 0: pl.ds(0, 8), 1: pl.ds(16, 8)}
+        block_in = {-1: 1, 0: 0, 1: 2}
+        order = sorted(range(26), key=lambda i: sum(map(abs, SIDES[i])))
+        for i in order:
+            dz, dx, dy = SIDES[i]
+            if dy == 0:
+                src = self.ext.at[pl.ds(0, 8), rows_out[dx], :]
+                dst = self.ext.at[planes_in[dz], rows_in[dx], :]
+            else:
+                land = self.left if dy == 1 else self.right
+                src = self.px.at[rows_out[dx], :]
+                dst = land.at[block_in[dz], rows_in[dx], :]
+            copy = pltpu.make_async_remote_copy(
+                src_ref=src,
+                dst_ref=dst,
+                send_sem=self.send.at[i],
+                recv_sem=self.recv.at[i],
+                device_id=neighbour(self.place, dz, dx, dy),
+                device_id_type=MESH,
+            )
+            copy.start()
+            self.copies.append(copy)
+
+    def finish(self):
+        at, size = self.place
+        for copy in self.copies:
+            copy.wait()
+        shape = (32, LANES)
+        row, lane = row_of(shape), lane_of(shape)
+        for block in range(3):
+            z_ok = (True, at["gz"] < size["gz"] - 1, at["gz"] > 0)[block]
+            ok = (row < 16) | ((row < 24) & (at["gx"] < size["gx"] - 1)) | ((row >= 24) & (at["gx"] > 0))
+            if block > 0:
+                ok = ok & z_ok
+            low = ok & (lane < 8) & (at["gy"] > 0)
+            high = ok & (lane >= 72) & (lane < 80) & (at["gy"] < size["gy"] - 1)
+            own = ok & (lane >= 8) & (lane < 72)
+            sides = jnp.where(lane % 16 < 8, self.left[block], self.right[block])
+            self.left[block] = sides
+
+            def body(i, carry, block=block, low=low, high=high, own=own):
+                z = 8 * block + i
+                sides = self.left[block]
+                merged = jnp.where(own, self.ext[z], 0.0)
+                merged = jnp.where(low, shift_lanes(sides, -16 * i), merged)
+                merged = jnp.where(high, shift_lanes(sides, 64 - 16 * i), merged)
+                self.ext[z] = merged
+                return carry
+
+            loop(8, body, 0)
+
+
+def neighbour(place, dz, dx, dy):
+    at, size = place
+    step = {"gz": dz, "gx": dx, "gy": dy}
+    return tuple(lax.rem(at[a] + step[a] + size[a], size[a]) if step[a] else at[a] for a in AXES)
+
+
 class Whole:
     def __init__(self, ext, shape):
         self.ext = ext
@@ -170,7 +285,7 @@
             weight = scale * (x + near[q])
             faces[q, z] = weight
             diagonal = diagonal + weight
-        inside = diagonal > 0.0
+        inside = x > 0.0
         rate[z] = jnp.where(inside, OMEGA / jnp.where(inside, diagonal, 1.0), 0.0)
         return carry
 
@@ -249,13 +364,17 @@
     at = {a: lax.axis_index(a) for a in AXES}
     place = (at, size)
 
-    def along(axis, step):
-        return tuple(lax.rem(at[a] + step, size[a]) if a == axis else at[a] for a in AXES)
-
+    peers = set()
+    for dz, dx, dy in SIDES:
+        peers.add((dz % size["gz"], dx % size["gx"], dy % size["gy"]))
+    peers.update((k, 0, 0) for k in range(1, size["gz"]))
+    flat = [(i, j) for i in range(size["gx"]) for j in range(size["gy"]) if (i, j) != (0, 0)]
+    peers.update((0, i, j) for i, j in flat)
     barrier = pltpu.get_barrier_semaphore()
-    peers = [(a, k) for a in AXES for k in range(1, size[a])]
-    for axis, step in peers:
-        pl.semaphore_signal(barrier, inc=1, device_id=along(axis, step), device_id_type=MESH)
+    for step in sorted(peers):
+        pl.semaphore_signal(
+            barrier, inc=1, device_id=neighbour(place, *step), device_id_type=MESH
+        )
 
     swaps = {}
     for k, name in enumerate(SWAP_FIELDS):
@@ -266,89 +385,164 @@
             int(name[1]),
             place,
         )
-
-    for level in range(4):
-        planes, rows = FINE[level]
-        if level > 0:
-            ref[f"s{level}"][...] = jnp.zeros(ref[f"s{level}"].shape, F32)
-            ref[f"k{level}"][...] = jnp.zeros(ref[f"k{level}"].shape, F32)
-            below = weight_ref if level == 1 else ref[f"k{level - 1}"]
-            restrict_weights(
-                lambda z, below=below: below[z],
-                2 * planes,
-                2 * rows,
-                2 ** (level - 1),
-                ref[f"k{level}"],
-                ref[f"t{level - 1}"],
-            )
-    ref["s4"][...] = jnp.zeros(ref["s4"].shape, F32)
-    ref["k4"][...] = jnp.zeros(ref["k4"].shape, F32)
-    restrict_weights(lambda z: ref["k3"][z], 2, 4, 8, ref["k4"], ref["t3"])
-    packed = {}
-    for level in range(4):
-        swap = swaps[f"w{level}"]
-        below = weight_ref if level == 0 else ref[f"k{level}"]
-        packed[level] = loop(
-            swap.planes,
-            lambda z, c, swap=swap, below=below: swap.put(z, below[z], c),
-            swap.empty(),
-        )
+    margins = {}
+    for k, name in enumerate(("w1", "s1")):
+        margins[name] = Margin(
+            *(ref[f"{name}{part}"] for part in ("", "_px", "_left", "_right")),
+            (ref["send_side"].at[k], ref["recv_side"].at[k]),
+            place,
+        )
+    square = (LANES, LANES)
+    to_ring = one_hot(row_of(square) == 2 * (lane_of(square) - MARGIN))
+
+    def into_ring(two_lanes, ring):
+        packed = exact_dot(two_lanes[...].reshape(LANES, LANES), to_ring)
+        ring[0:8, 0:16] = packed.reshape(8, 16, LANES)
+
+    swap = swaps["w0"]
+    packed = loop(16, lambda z, c: swap.put(z, weight_ref[z], c), swap.empty())
     pl.semaphore_wait(barrier, len(peers))
-    for level in range(4):
-        swaps[f"w{level}"].start(packed[level])
-    for level in range(4):
-        swap = swaps[f"w{level}"]
-        swap.finish()
-        face_weights(swap, ref[f"f{level}"], ref[f"d{level}"], level)
-
-    sources = [source_ref, ref["s1"], ref["s2"], ref["s3"], ref["s4"]]
-    for level in range(4):
-        swap = swaps[f"v{level}"]
-        swap.start(first_relax(swap, sources[level], ref[f"d{level}"], swap.empty()))
-        swap.finish()
-        down(swap, sources[level], ref[f"f{level}"], 2**level, sources[level + 1], ref[f"t{level}"])
+    swap.start(packed)
+    restrict_weights(lambda z: weight_ref[z], 16, 32, 1, ref["k1"], ref["t0"])
+    into_ring(ref["k1"], ref["w1"])
+    margins["w1"].start()
+    swap.finish()
+    face_weights(swap, ref["f0"], ref["d0"], 0)
+    swap = swaps["v0"]
+    swap.start(first_relax(swap, source_ref, ref["d0"], swap.empty()))
+
+    margins["w1"].finish()
+    rings = {}
+    for level in (1, 2, 3):
+        for kind in "wvc":
+            rings[kind, level] = Ring(ref[f"{kind}{level}"], level)
+        field = rings["w", level]
+        face_weights(field, ref[f"f{level}"], ref[f"d{level}"], level)
+        target = ref[f"w{level + 1}"] if level < 3 else ref["k4"]
+        planes = field.planes if level < 3 else 2
+        restrict_weights(
+            lambda z, field=field: field.ext[z], planes, field.rows, field.half, target, ref[f"t{level}"]
+        )
+    swap.finish()
+    down(swap, source_ref, ref["f0"], 1, ref["k1"], ref["t0"])
+    into_ring(ref["k1"], ref["s1"])
+    margins["s1"].start()
+    margins["s1"].finish()
+
+    spans = {1: ((0, 24), (9, 10)), 2: ((9, 10), (5, 4)), 3: ((5, 4), (0, 1))}
+    for level in (1, 2, 3):
+        field, faces, rate = rings["v", level], ref[f"f{level}"], ref[f"d{level}"]
+        source = ref[f"s{level}"]
+        (first, count), (low, pairs) = spans[level]
+
+        def relax_plane(z, field=field, rate=rate, source=source):
+            field.put(z, rate[z] * source[z], 0)
+
+        ring_loop(first, count, field.planes, relax_plane)
+
+        def pair(z, field=field, faces=faces, source=source, level=level):
+            total = None
+            for part in range(2):
+                i = 2 * z + part
+                defect = source[i] - applied(field.around(i), faces, i)
+                total = defect if total is None else total + defect
+            below = pair_down(total, field.rows, field.half, ref[f"t{level}"])
+            store_layer(ref[f"s{level + 1}"], z, below)
+
+        ring_loop(low, pairs, field.planes // 2, pair)
 
     tile = (8, LANES)
     lane, row = lane_of(tile), row_of(tile)
     own = jnp.concatenate([ref["s4"][0][0:2], ref["k4"][0][0:2], jnp.zeros((4, LANES), F32)], 0)
-    square = (LANES, LANES)
-    pick = one_hot(row_of(square) == lane_of(square) % 8 * 16)
+    pick = one_hot(row_of(square) == MARGIN + lane_of(square) % 8 * 8)
     shrunk = exact_dot(own, pick)
     line = jnp.sum(jnp.where(lane // 32 == row, shrunk, 0.0), axis=0, keepdims=True)
     ref["g0"][...] = line
 
-    def all_to_all(axis, src, dst, send, recv):
-        copies = []
-        for step in range(1, size[axis]):
-            copy = pltpu.make_async_remote_copy(
-                src_ref=src,
-                dst_ref=dst.at[at[axis]],
-                send_sem=send.at[step],
-                recv_sem=recv.at[step],
-                device_id=along(axis, step),
-                device_id_type=MESH,
-            )
-            copy.start()
-            copies.append(copy)
-        dst[at[axis]] = src[...]
-        for copy in copies:
-            copy.wait()
-
-    all_to_all("gy", ref["g0"], ref["g1"], ref["send_gy"], ref["recv_gy"])
-    lane1 = lane_of((1, LANES))
-    merged = jnp.zeros((1, LANES), F32)
+    copies = []
+
+    def send(src, dst, key, i, step):
+        copy = pltpu.make_async_remote_copy(
+            src_ref=src,
+            dst_ref=dst,
+            send_sem=ref[f"send_{key}"].at[i],
+            recv_sem=ref[f"recv_{key}"].at[i],
+            device_id=neighbour(place, *step),
+            device_id_type=MESH,
+        )
+        copy.start()
+        return copy
+
+    for i, (dx, dy) in enumerate(flat):
+        copies.append(send(ref["g0"], ref["g1"].at[at["gy"], at["gx"]], "flat", i, (0, dx, dy)))
+    ref["g1"][at["gy"], at["gx"]] = line
+
+    def stacked(name):
+        return jnp.where(row < 4, ref[name][0], pltpu.roll(ref[name][1], 4, 0))
+
+    ref["own3"][...] = jnp.where(
+        lane < 64, shift_lanes(stacked("s3"), -MARGIN), shift_lanes(stacked("d3"), 64 - MARGIN)
+    )
+    side_copies = [
+        send(ref["own3"], ref["side3"].at[i], "side3", i, SIDES[i]) for i in range(26)
+    ]
+    for copy in copies:
+        copy.wait()
+    merged = jnp.zeros(tile, F32)
     for k in range(size["gy"]):
-        merged = jnp.where(lane1 // 8 % 4 == k, ref["g1"][k], merged)
+        rows = jnp.concatenate([ref["g1"][k, i] for i in range(size["gx"])], 0)
+        merged = jnp.where(lane // 8 % 4 == k, rows, merged)
     ref["g2"][...] = merged
-    all_to_all("gz", ref["g2"], ref["g3"], ref["send_gz"], ref["recv_gz"])
-    all_to_all("gx", ref["g3"], ref["g4"], ref["send_gx"], ref["recv_gx"])
+    copies = [
+        send(ref["g2"], ref["g5"].at[at["gz"]], "gz", k, (k, 0, 0)) for k in range(1, size["gz"])
+    ]
+    ref["g5"][at["gz"]] = merged
+
+    for copy in side_copies:
+        copy.wait()
+    inside = {
+        "gz": {0: True, 1: at["gz"] < size["gz"] - 1, -1: at["gz"] > 0},
+        "gx": {0: True, 1: at["gx"] < size["gx"] - 1, -1: at["gx"] > 0},
+        "gy": {0: True, 1: at["gy"] < size["gy"] - 1, -1: at["gy"] > 0},
+    }
+
+    def from_side(dz, dx, dy):
+        if (dz, dx, dy) == (0, 0, 0):
+            return ref["own3"][...]
+        x = ref["side3"][SIDES.index((-dz, -dx, -dy))]
+        for axis, step in (("gz", dz), ("gx", dx), ("gy", dy)):
+            if step:
+                x = jnp.where(inside[axis][step], x, 0.0)
+        return x
+
+    for block, dz in enumerate((0, 1, -1)):
+        column = {}
+        for dy in (-1, 0, 1):
+            mid, up, low = (from_side(dz, dx, dy) for dx in (0, 1, -1))
+            turn = lambda x: pltpu.roll(x, 4, 0)
+            far = jnp.where(row < 6, turn(up), turn(low))
+            column[0, dy] = jnp.where(row < 4, mid, far)
+            far = jnp.where(row < 6, up, low)
+            column[1, dy] = jnp.where(row < 4, turn(mid), far)
+        for part in range(2):
+            z = 2 * block + part
+            mid = column[part, 0]
+            for name, base in (("s3", 0), ("d3", 64)):
+                ends = jnp.where(
+                    lane < 8,
+                    shift_lanes(column[part, -1], 72 - base),
+                    shift_lanes(column[part, 1], 72 - base),
+                )
+                body = shift_lanes(mid, MARGIN - base)
+                full = jnp.where((lane >= 8) & (lane < 72), body, jnp.where(lane < 80, ends, 0.0))
+                ref[name][z] = full
+            rings["v", 3].put(z, ref["d3"][z] * ref["s3"][z], 0)
+    for copy in copies:
+        copy.wait()
 
     wide = (LANES, 4 * LANES)
     expand = one_hot(row_of(wide) == lane_of(wide) // LANES * 32 + lane_of(wide) % LANES // 4)
-    for z in range(size["gz"]):
-        for k in range(size["gx"]):
-            ref["g5"][8 * z + k : 8 * z + k + 1, :] = ref["g4"][k, z]
-    ref["g6"][...] = exact_dot(ref["g5"][...], expand)
+    ref["g6"][...] = exact_dot(ref["g5"][...].reshape(LANES, LANES), expand)
     fields = {}
     for level in range(4, 7):
         for kind in "wvc":
@@ -410,42 +604,80 @@
 
         relax_into(field, ref[f"q{level}"], ref[f"f{level}"], ref[f"d{level}"], put, 0)
 
-    pick_lane = one_hot(row_of(square) == (8 * at["gy"] + lane_of(square) // 16) * 4)
-    pick_row = one_hot(lane_of((8, 16)) == 2 * at["gx"] + row_of((8, 16)))
-    mine = exact_dot(pick_row, exact_dot(ref["e4"][at["gz"]], pick_lane))
-    ref["e_own"][...] = mine
-
-    coarse_layer = lambda z: ref["e_own"][...]
-    for level in (3, 2, 1, 0):
-        swap = swaps[f"c{level}"]
-        old = swaps[f"v{level}"]
-        swap.start(add_coarse(swap, old, coarse_layer, swap.empty(), ref[f"t{level}"]))
-        swap.finish()
-        source, faces, rate = sources[level], ref[f"f{level}"], ref[f"d{level}"]
-        if level > 0:
-            target = ref[f"e{level}"]
-
-            def put(z, x, carry, target=target):
-                target[z] = x
-                return carry
-
-            relax_into(swap, source, faces, rate, put, 0)
-            coarse_layer = lambda z, target=target: target[z]
-        else:
-            last = swaps["r0"]
-
-            def put(z, x, carry):
-                out_ref[z] = x
-                return last.put(z, x, carry)
-
-            last.start(relax_into(swap, source, faces, rate, put, last.empty()))
-            last.finish()
-
-            def body(z, carry):
-                residual_ref[z] = source[z] - applied(last.around(z), faces, z)
-                return carry
-
-            loop(16, body, 0)
+    pick_lane = one_hot(row_of(square) == (8 * at["gy"] - 1 + lane_of(square) // 8) * 4)
+    coarse_row = (row_of((8, 16)) // 2 + 1) % 4 - 1
+    pick_row = one_hot(lane_of((8, 16)) == 2 * at["gx"] + coarse_row)
+    for block, dz in enumerate((0, 1, -1)):
+        layer = ref["e4"][jnp.clip(at["gz"] + dz, 0, size["gz"] - 1)]
+        if dz:
+            layer = jnp.where(inside["gz"][dz], layer, 0.0)
+        up = exact_dot(pick_row, exact_dot(layer, pick_lane))
+        for part in range(2):
+            z = 2 * block + part
+            rings["c", 3].put(z, rings["v", 3].ext[z] + up, 0)
+
+    for level, first, count in ((3, 5, 4), (2, 11, 6), (1, 23, 10)):
+        field, faces, rate = rings["c", level], ref[f"f{level}"], ref[f"d{level}"]
+        source, target = ref[f"s{level}"], ref[f"e{level}"]
+        if level < 3:
+            coarse, scratch = ref[f"e{level + 1}"], ref[f"t{level}"]
+
+            def lift(z, field=field, coarse=coarse, scratch=scratch, level=level):
+                wide = spread(coarse[z], field.rows, scratch)
+                for part in range(2):
+                    i = 2 * z + part
+                    field.put(i, rings["v", level].ext[i] + wide, 0)
+
+            ring_loop(first // 2, (count + 2) // 2, field.planes // 2, lift)
+
+        def relax_plane(z, field=field, faces=faces, rate=rate, source=source, target=target):
+            around = field.around(z)
+            target[z] = around[0] + rate[z] * (source[z] - applied(around, faces, z))
+
+        ring_loop(first, count, field.planes, relax_plane)
+
+    to_fine = one_hot(row_of(square) == MARGIN + lane_of(square) // 2)
+    swap, old = swaps["c0"], swaps["v0"]
+    scratch = ref["t1w"]
+    side = old.side[...]
+
+    def lifted(zc):
+        return spread(exact_dot(ref["e1"][zc], to_fine), 0, scratch)
+
+    def lift(zc, side):
+        layer = ref["e1"][zc]
+        wide = spread(exact_dot(layer, to_fine), 0, scratch)
+        at_lane = lane_of(square) // 4 == zc
+        ends = one_hot(
+            at_lane
+            & (row_of(square) == jnp.where(lane_of(square) % 2 == 0, MARGIN - 1, MARGIN + 64))
+        )
+        side = side + spread(exact_dot(layer, ends), 0, scratch)[0:32]
+        for part in range(2):
+            i = 2 * zc + part
+            swap.ext[i + 1] = old.ext[i + 1] + wide[0:32]
+            swap.yhi[i] = old.yhi[i] + jnp.where(inside["gx"][1], wide[32:33], 0.0)
+            swap.ylo[i] = old.ylo[i] + jnp.where(inside["gx"][-1], wide[63:64], 0.0)
+        return side
+
+    swap.side[...] = loop(8, lift, side)
+    swap.ext[17] = old.ext[17] + lifted(8)[0:32]
+    swap.ext[0] = old.ext[0] + lifted(23)[0:32]
+    last = swaps["r0"]
+    faces, rate = ref["f0"], ref["d0"]
+
+    def put(z, x, carry):
+        out_ref[z] = x
+        return last.put(z, x, carry)
+
+    last.start(relax_into(swap, source_ref, faces, rate, put, last.empty()))
+    last.finish()
+
+    def body(z, carry):
+        residual_ref[z] = source_ref[z] - applied(last.around(z), faces, z)
+        return carry
+
+    loop(16, body, 0)
 
 
 def buffers(size):
@@ -462,18 +694,24 @@
             vmem(f"{name}_{part}", planes, 1, LANES)
         for part in ("px", "xlo", "xhi", "side"):
             vmem(f"{name}_{part}", tall, LANES)
-    for level, (planes, rows) in enumerate(FINE):
-        tall = padded_rows(rows)
-        vmem(f"f{level}", 6, planes, tall, LANES)
-        vmem(f"d{level}", planes, tall, LANES)
-        vmem(f"t{level}", tall, LANES)
-        if level > 0:
-            vmem(f"s{level}", planes, tall, LANES)
-            vmem(f"k{level}", planes, tall, LANES)
-            vmem(f"e{level}", planes, tall, LANES)
-    vmem("s4", 1, 8, LANES)
-    vmem("k4", 1, 8, LANES)
-    vmem("e_own", 8, LANES)
+    vmem("f0", 6, 16, 32, LANES)
+    vmem("d0", 16, 32, LANES)
+    vmem("t0", 32, LANES)
+    vmem("t1w", 64, LANES)
+    vmem("k1", 8, 16, LANES)
+    for level, (planes, rows, _) in RING.items():
+        for kind in "wsvced":
+            vmem(f"{kind}{level}", planes, rows, LANES)
+        vmem(f"f{level}", 6, planes, rows, LANES)
+        vmem(f"t{level}", rows, LANES)
+    for name in ("w1", "s1"):
+        vmem(f"{name}_px", 16, LANES)
+        vmem(f"{name}_left", 3, 32, LANES)
+        vmem(f"{name}_right", 3, 32, LANES)
+    vmem("s4", 1, 4, LANES)
+    vmem("k4", 1, 4, LANES)
+    vmem("own3", 8, LANES)
+    vmem("side3", 26, 8, LANES)
     for level, (planes, rows, _) in zip((4, 5, 6), COARSE):
         tall = padded_rows(rows)
         for kind in "wvc":
@@ -486,17 +724,17 @@
         if level > 4:
             vmem(f"k{level}", planes, tall, LANES)
     vmem("g0", 1, LANES)
-    vmem("g1", size["gy"], 1, LANES)
-    vmem("g2", 1, LANES)
-    vmem("g3", size["gz"], 1, LANES)
-    vmem("g4", size["gx"], size["gz"], 1, LANES)
-    vmem("g5", size["gx"] * size["gz"], LANES)
+    vmem("g1", size["gy"], size["gx"], 1, LANES)
+    vmem("g2", 8, LANES)
+    vmem("g5", size["gz"], 8, LANES)
     vmem("g6", size["gx"] * size["gz"], 4 * LANES)
     shapes["send"] = pltpu.SemaphoreType.DMA((len(SWAP_FIELDS), 6))
     shapes["recv"] = pltpu.SemaphoreType.DMA((len(SWAP_FIELDS), 6))
-    for axis in AXES:
-        shapes[f"send_{axis}"] = pltpu.SemaphoreType.DMA((size[axis],))
-        shapes[f"recv_{axis}"] = pltpu.SemaphoreType.DMA((size[axis],))
+    shapes["send_side"] = pltpu.SemaphoreType.DMA((2, 26))
+    shapes["recv_side"] = pltpu.SemaphoreType.DMA((2, 26))
+    for key, count in (("flat", size["gx"] * size["gy"]), ("side3", 26), ("gz", size["gz"])):
+        shapes[f"send_{key}"] = pltpu.SemaphoreType.DMA((count,))
+        shapes[f"recv_{key}"] = pltpu.SemaphoreType.DMA((count,))
     return shapes
 
 

time: 81.6 us -> 68.7 us (0.84)
  Pallas kernels: 77.5 us -> 64.6 us
    pallas_call x1, Pallas kernels: 77.5 us -> 64.6 us  [body(): pl.pallas_call(run, out_shape=(block, block), in_specs=[pl.BlockSpec(memo...]
where the time goes in v2:
time: 68.7 us; the launch traced here: 68.5 us
  Pallas kernels  64.6 us (94%)
  local copies, waits for them, and re-layouts  3.3 us (5%)
    pallas_call x1, Pallas kernels, body(): pl.pallas_call(run, out_shape=(block, block), in_specs=[pl.BlockSpec(memo...  64.6 us
    unnamed x6, local copies, waits for them, and re-layouts  3.3 us

profile of v2, /device:TPU:1, one launch (start us, length us, event | category | flops | bytes accessed | tf_op | source)
XLA Modules:
  0.0 68.5 jit_solution(3614609425812516793)
XLA Ops:
  0.6 0.0 copy-start
  0.6 0.9 %copy-done = f32[16,32,128]{2,1,0:T(8,128)S(1)} copy-done((f32[16,32,128]{2,1,0:T(8,128)S(1)}, f32[16,32,128]{2,1,0:T(8,128)}, u32[]{:S(2)}) %copy-start) | copy-done | bytes 262168
  1.6 0.0 copy-start.1
  1.6 0.9 %copy-done.1 = f32[16,32,128]{2,1,0:T(8,128)S(1)} copy-done((f32[16,32,128]{2,1,0:T(8,128)S(1)}, f32[16,32,128]{2,1,0:T(8,128)}, u32[]{:S(2)}) %copy-start.1) | copy-done | bytes 262168
  2.5 64.6 %shard_map.41 = (f32[16,32,128]{2,1,0:T(8,128)S(1)}, f32[16,32,128]{2,1,0:T(8,128)S(1)}) custom-call(f32[16,32,128]{2,1,0:T(8,128)S(1)} %copy-done, f32[16,32,128]{2,1,0:T(8,128)S(1)} %copy-done.1), custom_call_target="tpu_custom_call" | custom-call | tf_op jit(solution)/shard_map/pallas_call | solution.py:752
  67.1 0.7 %copy.6 = f32[16,32,128]{2,1,0:T(8,128)} copy(f32[16,32,128]{2,1,0:T(8,128)S(1)} %get-tuple-element.4) | data formatting | bytes 524288
  67.8 0.7 %copy.7 = f32[16,32,128]{2,1,0:T(8,128)} copy(f32[16,32,128]{2,1,0:T(8,128)S(1)} %get-tuple-element.5) | data formatting | bytes 524288
Async XLA Ops:
  0.6 1.0 %copy-start = (f32[16,32,128]{2,1,0:T(8,128)S(1)}, f32[16,32,128]{2,1,0:T(8,128)}, u32[]{:S(2)}) copy-start(f32[16,32,128]{2,1,0:T(8,128)} %refs_0_.1) | copy-start | bytes 786436
  1.6 0.9 %copy-start.1 = (f32[16,32,128]{2,1,0:T(8,128)S(1)}, f32[16,32,128]{2,1,0:T(8,128)}, u32[]{:S(2)}) copy-start(f32[16,32,128]{2,1,0:T(8,128)} %refs_1_.1) | copy-start | bytes 786436

commit v3 on v2

--- a/solution.py
+++ b/solution.py
@@ -359,14 +359,15 @@
     loop(planes // 2, body, 0)
 
 
-def kernel(size, names, source_ref, weight_ref, out_ref, residual_ref, *scratch):
+def kernel(size, names, source_hbm, weight_hbm, out_ref, residual_ref, *scratch):
     ref = dict(zip(names, scratch))
+    source_ref, weight_ref = ref["source"], ref["weight"]
+    load_weight = pltpu.make_async_copy(weight_hbm, weight_ref, ref["load"].at[0])
+    load_source = pltpu.make_async_copy(source_hbm, source_ref, ref["load"].at[1])
     at = {a: lax.axis_index(a) for a in AXES}
     place = (at, size)
 
     peers = set()
-    for dz, dx, dy in SIDES:
-        peers.add((dz % size["gz"], dx % size["gx"], dy % size["gy"]))
     peers.update((k, 0, 0) for k in range(1, size["gz"]))
     flat = [(i, j) for i in range(size["gx"]) for j in range(size["gy"]) if (i, j) != (0, 0)]
     peers.update((0, i, j) for i, j in flat)
@@ -375,6 +376,8 @@
         pl.semaphore_signal(
             barrier, inc=1, device_id=neighbour(place, *step), device_id_type=MESH
         )
+    load_weight.start()
+    load_source.start()
 
     swaps = {}
     for k, name in enumerate(SWAP_FIELDS):
@@ -399,34 +402,112 @@
         packed = exact_dot(two_lanes[...].reshape(LANES, LANES), to_ring)
         ring[0:8, 0:16] = packed.reshape(8, 16, LANES)
 
+    tile = (8, LANES)
+    lane, row = lane_of(tile), row_of(tile)
+
+    def send(src, dst, key, i, step):
+        copy = pltpu.make_async_remote_copy(
+            src_ref=src,
+            dst_ref=dst,
+            send_sem=ref[f"send_{key}"].at[i],
+            recv_sem=ref[f"recv_{key}"].at[i],
+            device_id=neighbour(place, *step),
+            device_id_type=MESH,
+        )
+        copy.start()
+        return copy
+
+    def gather_flat(kind, rows, first, width):
+        own = jnp.concatenate([rows, jnp.zeros((6, LANES), F32)], 0)
+        pick = one_hot(row_of(square) == first + lane_of(square) % 8 * width)
+        shrunk = exact_dot(own, pick)
+        line = jnp.sum(jnp.where(lane // 32 == row, shrunk, 0.0), axis=0, keepdims=True)
+        src, dst = ref[f"g0{kind}"], ref[f"g1{kind}"]
+        src[...] = line
+        copies = [
+            send(src, dst.at[at["gy"], at["gx"]], f"flat_{kind}", i, (0, dx, dy))
+            for i, (dx, dy) in enumerate(flat)
+        ]
+        dst[at["gy"], at["gx"]] = line
+        return copies
+
+    def gather_gz(kind, copies):
+        for copy in copies:
+            copy.wait()
+        lines, src, dst = ref[f"g1{kind}"], ref[f"g2{kind}"], ref[f"g5{kind}"]
+        merged = jnp.zeros(tile, F32)
+        for k in range(size["gy"]):
+            rows = jnp.concatenate([lines[k, i] for i in range(size["gx"])], 0)
+            merged = jnp.where(lane // 8 % 4 == k, rows, merged)
+        src[...] = merged
+        copies = [
+            send(src, dst.at[at["gz"]], f"gz_{kind}", k, (k, 0, 0)) for k in range(1, size["gz"])
+        ]
+        dst[at["gz"]] = merged
+        return copies
+
+    def gather_end(kind, copies, target, first):
+        for copy in copies:
+            copy.wait()
+        wide = (LANES, 2 * LANES)
+        expand = one_hot(row_of(wide) == lane_of(wide) // LANES * 32 + lane_of(wide) % LANES // 4)
+        ref["g6"][...] = exact_dot(ref[f"g5{kind}"][...].reshape(LANES, LANES), expand)
+
+        def body(z, carry):
+            block = ref["g6"][pl.ds(pl.multiple_of(8 * z, 8), 8), :]
+            for part in range(2):
+                rows = pl.ds(part, 8, stride=2)
+                target[z + first, rows, :] = block[:, part * LANES : (part + 1) * LANES]
+            return carry
+
+        loop(16, body, 0)
+
     swap = swaps["w0"]
+    load_weight.wait()
     packed = loop(16, lambda z, c: swap.put(z, weight_ref[z], c), swap.empty())
     pl.semaphore_wait(barrier, len(peers))
     swap.start(packed)
     restrict_weights(lambda z: weight_ref[z], 16, 32, 1, ref["k1"], ref["t0"])
     into_ring(ref["k1"], ref["w1"])
-    margins["w1"].start()
+    restrict_weights(lambda z: ref["k1"][z], 8, 16, 2, ref["h2"], ref["u1"])
+    restrict_weights(lambda z: ref["h2"][z], 4, 8, 4, ref["h3"], ref["u2"])
+    restrict_weights(lambda z: ref["h3"][z], 2, 4, 8, ref["h4"], ref["u3"])
+    load_source.wait()
     swap.finish()
     face_weights(swap, ref["f0"], ref["d0"], 0)
     swap = swaps["v0"]
     swap.start(first_relax(swap, source_ref, ref["d0"], swap.empty()))
-
-    margins["w1"].finish()
+    copies_w = gather_flat("w", ref["h4"][0], 0, 16)
+    margins["w1"].start()
     rings = {}
     for level in (1, 2, 3):
         for kind in "wvc":
             rings[kind, level] = Ring(ref[f"{kind}{level}"], level)
-        field = rings["w", level]
-        face_weights(field, ref[f"f{level}"], ref[f"d{level}"], level)
-        target = ref[f"w{level + 1}"] if level < 3 else ref["k4"]
-        planes = field.planes if level < 3 else 2
-        restrict_weights(
-            lambda z, field=field: field.ext[z], planes, field.rows, field.half, target, ref[f"t{level}"]
-        )
+    fields = {}
+    for level in range(4, 7):
+        for kind in "wvc":
+            fields[kind, level] = Whole(ref[f"{kind}{level}_ext"], COARSE[level - 4])
+    ref["k6"][...] = jnp.zeros(ref["k6"].shape, F32)
+    ref["q6"][...] = jnp.zeros(ref["q6"].shape, F32)
     swap.finish()
     down(swap, source_ref, ref["f0"], 1, ref["k1"], ref["t0"])
     into_ring(ref["k1"], ref["s1"])
     margins["s1"].start()
+
+    copies_w = gather_gz("w", copies_w)
+    margins["w1"].finish()
+    for level in (1, 2, 3):
+        field = rings["w", level]
+        face_weights(field, ref[f"f{level}"], ref[f"d{level}"], level)
+        if level < 3:
+            restrict_weights(
+                lambda z, field=field: field.ext[z],
+                field.planes,
+                field.rows,
+                field.half,
+                ref[f"w{level + 1}"],
+                ref[f"t{level}"],
+            )
     margins["s1"].finish()
 
     spans = {1: ((0, 24), (9, 10)), 2: ((9, 10), (5, 4)), 3: ((5, 4), (0, 1))}
@@ -451,31 +532,7 @@
 
         ring_loop(low, pairs, field.planes // 2, pair)
 
-    tile = (8, LANES)
-    lane, row = lane_of(tile), row_of(tile)
-    own = jnp.concatenate([ref["s4"][0][0:2], ref["k4"][0][0:2], jnp.zeros((4, LANES), F32)], 0)
-    pick = one_hot(row_of(square) == MARGIN + lane_of(square) % 8 * 8)
-    shrunk = exact_dot(own, pick)
-    line = jnp.sum(jnp.where(lane // 32 == row, shrunk, 0.0), axis=0, keepdims=True)
-    ref["g0"][...] = line
-
-    copies = []
-
-    def send(src, dst, key, i, step):
-        copy = pltpu.make_async_remote_copy(
-            src_ref=src,
-            dst_ref=dst,
-            send_sem=ref[f"send_{key}"].at[i],
-            recv_sem=ref[f"recv_{key}"].at[i],
-            device_id=neighbour(place, *step),
-            device_id_type=MESH,
-        )
-        copy.start()
-        return copy
-
-    for i, (dx, dy) in enumerate(flat):
-        copies.append(send(ref["g0"], ref["g1"].at[at["gy"], at["gx"]], "flat", i, (0, dx, dy)))
-    ref["g1"][at["gy"], at["gx"]] = line
+    copies_s = gather_flat("s", ref["s4"][0][0:2], MARGIN, 8)
 
     def stacked(name):
         return jnp.where(row < 4, ref[name][0], pltpu.roll(ref[name][1], 4, 0))
@@ -486,17 +543,19 @@
     side_copies = [
         send(ref["own3"], ref["side3"].at[i], "side3", i, SIDES[i]) for i in range(26)
     ]
-    for copy in copies:
-        copy.wait()
-    merged = jnp.zeros(tile, F32)
-    for k in range(size["gy"]):
-        rows = jnp.concatenate([ref["g1"][k, i] for i in range(size["gx"])], 0)
-        merged = jnp.where(lane // 8 % 4 == k, rows, merged)
-    ref["g2"][...] = merged
-    copies = [
-        send(ref["g2"], ref["g5"].at[at["gz"]], "gz", k, (k, 0, 0)) for k in range(1, size["gz"])
-    ]
-    ref["g5"][at["gz"]] = merged
+    gather_end("w", copies_w, ref["w4_ext"], 1)
+    for level in (4, 5):
+        planes, rows, half = COARSE[level - 4]
+        field = fields["w", level]
+        target = ref[f"k{level + 1}"]
+        restrict_weights(
+            lambda z, field=field: field.ext[z + 1], planes, rows, half, target, ref[f"t{level}"]
+        )
+        for z in range(planes // 2):
+            fields["w", level + 1].put(z, target[z], 0)
+    for level in (4, 5, 6):
+        face_weights(fields["w", level], ref[f"f{level}"], ref[f"d{level}"], level)
+    copies_s = gather_gz("s", copies_s)
 
     for copy in side_copies:
         copy.wait()
@@ -537,37 +596,8 @@
                 full = jnp.where((lane >= 8) & (lane < 72), body, jnp.where(lane < 80, ends, 0.0))
                 ref[name][z] = full
             rings["v", 3].put(z, ref["d3"][z] * ref["s3"][z], 0)
-    for copy in copies:
-        copy.wait()
-
-    wide = (LANES, 4 * LANES)
-    expand = one_hot(row_of(wide) == lane_of(wide) // LANES * 32 + lane_of(wide) % LANES // 4)
-    ref["g6"][...] = exact_dot(ref["g5"][...].reshape(LANES, LANES), expand)
-    fields = {}
-    for level in range(4, 7):
-        for kind in "wvc":
-            fields[kind, level] = Whole(ref[f"{kind}{level}_ext"], COARSE[level - 4])
-    for z in range(16):
-        block = ref["g6"][8 * z : 8 * z + 8, :]
-        for part in range(2):
-            rows = pl.ds(part, 8, stride=2)
-            ref["q4"][z, rows, :] = block[:, part * LANES : (part + 1) * LANES]
-            ref["w4_ext"][z + 1, rows, :] = block[:, (part + 2) * LANES : (part + 3) * LANES]
-
-    for level in (4, 5):
-        planes, rows, half = COARSE[level - 4]
-        field = fields["w", level]
-        if level == 5:
-            ref["k6"][...] = jnp.zeros(ref["k6"].shape, F32)
-            ref["q6"][...] = jnp.zeros(ref["q6"].shape, F32)
-        target = ref[f"k{level + 1}"]
-        restrict_weights(
-            lambda z, field=field: field.ext[z + 1], planes, rows, half, target, ref[f"t{level}"]
-        )
-        for z in range(planes // 2):
-            fields["w", level + 1].put(z, target[z], 0)
-    for level in (4, 5, 6):
-        face_weights(fields["w", level], ref[f"f{level}"], ref[f"d{level}"], level)
+    gather_end("s", copies_s, ref["q4"], 0)
+
     for level in (4, 5):
         field, faces = fields["v", level], ref[f"f{level}"]
         first_relax(field, ref[f"q{level}"], ref[f"d{level}"], 0)
@@ -709,7 +739,11 @@
         vmem(f"{name}_left", 3, 32, LANES)
         vmem(f"{name}_right", 3, 32, LANES)
     vmem("s4", 1, 4, LANES)
-    vmem("k4", 1, 4, LANES)
+    vmem("source", 16, 32, LANES)
+    vmem("weight", 16, 32, LANES)
+    for level, rows in ((2, 8), (3, 4), (4, 2)):
+        vmem(f"h{level}", 16 >> level, rows, LANES)
+        vmem(f"u{level - 1}", 2 * rows, LANES)
     vmem("own3", 8, LANES)
     vmem("side3", 26, 8, LANES)
     for level, (planes, rows, _) in zip((4, 5, 6), COARSE):
@@ -723,16 +757,21 @@
         vmem(f"t{level}", tall, LANES)
         if level > 4:
             vmem(f"k{level}", planes, tall, LANES)
-    vmem("g0", 1, LANES)
-    vmem("g1", size["gy"], size["gx"], 1, LANES)
-    vmem("g2", 8, LANES)
-    vmem("g5", size["gz"], 8, LANES)
-    vmem("g6", size["gx"] * size["gz"], 4 * LANES)
+    for kind in "ws":
+        vmem(f"g0{kind}", 1, LANES)
+        vmem(f"g1{kind}", size["gy"], size["gx"], 1, LANES)
+        vmem(f"g2{kind}", 8, LANES)
+        vmem(f"g5{kind}", size["gz"], 8, LANES)
+    vmem("g6", size["gx"] * size["gz"], 2 * LANES)
+    shapes["load"] = pltpu.SemaphoreType.DMA((2,))
     shapes["send"] = pltpu.SemaphoreType.DMA((len(SWAP_FIELDS), 6))
     shapes["recv"] = pltpu.SemaphoreType.DMA((len(SWAP_FIELDS), 6))
     shapes["send_side"] = pltpu.SemaphoreType.DMA((2, 26))
     shapes["recv_side"] = pltpu.SemaphoreType.DMA((2, 26))
-    for key, count in (("flat", size["gx"] * size["gy"]), ("side3", 26), ("gz", size["gz"])):
+    counts = [("side3", 26)]
+    for kind in "ws":
+        counts += [(f"flat_{kind}", size["gx"] * size["gy"]), (f"gz_{kind}", size["gz"])]
+    for key, count in counts:
         shapes[f"send_{key}"] = pltpu.SemaphoreType.DMA((count,))
         shapes[f"recv_{key}"] = pltpu.SemaphoreType.DMA((count,))
     return shapes
@@ -752,7 +791,7 @@
         return pl.pallas_call(
             run,
             out_shape=(block, block),
-            in_specs=[pl.BlockSpec(memory_space=pltpu.VMEM)] * 2,
+            in_specs=[pl.BlockSpec(memory_space=pltpu.HBM)] * 2,
             out_specs=[pl.BlockSpec(memory_space=pltpu.VMEM)] * 2,
             scratch_shapes=list(shapes.values()),
             compiler_params=pltpu.CompilerParams(

time: 68.7 us -> 65.2 us (0.949)
  Pallas kernels: 64.6 us -> 61.1 us
    pallas_call x1, Pallas kernels: 64.6 us -> 61.1 us  [body(): pl.pallas_call(run, out_shape=(block, block), in_specs=[pl.BlockSpec(memo...]
where the time goes in v3:
time: 65.2 us; the launch traced here: 65 us
  Pallas kernels  61.1 us (94%)
  local copies, waits for them, and re-layouts  3.3 us (5%)
    pallas_call x1, Pallas kernels, body(): pl.pallas_call(run, out_shape=(block, block), in_specs=[pl.BlockSpec(memo...  61.1 us
    unnamed x6, local copies, waits for them, and re-layouts  3.3 us

profile of v3, /device:TPU:1, one launch (start us, length us, event | category | flops | bytes accessed | tf_op | source)
XLA Modules:
  0.0 65.0 jit_solution(9498273031664964464)
XLA Ops:
  0.6 0.0 copy-start
  0.6 0.9 %copy-done = f32[16,32,128]{2,1,0:T(8,128)S(1)} copy-done((f32[16,32,128]{2,1,0:T(8,128)S(1)}, f32[16,32,128]{2,1,0:T(8,128)}, u32[]{:S(2)}) %copy-start) | copy-done | bytes 262168
  1.6 0.0 copy-start.1
  1.6 0.9 %copy-done.1 = f32[16,32,128]{2,1,0:T(8,128)S(1)} copy-done((f32[16,32,128]{2,1,0:T(8,128)S(1)}, f32[16,32,128]{2,1,0:T(8,128)}, u32[]{:S(2)}) %copy-start.1) | copy-done | bytes 262168
  2.5 61.1 %shard_map.41 = (f32[16,32,128]{2,1,0:T(8,128)S(1)}, f32[16,32,128]{2,1,0:T(8,128)S(1)}) custom-call(f32[16,32,128]{2,1,0:T(8,128)S(1)} %copy-done, f32[16,32,128]{2,1,0:T(8,128)S(1)} %copy-done.1), custom_call_target="tpu_custom_call" | custom-call | tf_op jit(solution)/shard_map/pallas_call | solution.py:791
  63.6 0.7 %copy.6 = f32[16,32,128]{2,1,0:T(8,128)} copy(f32[16,32,128]{2,1,0:T(8,128)S(1)} %get-tuple-element.4) | data formatting | bytes 524288
  64.3 0.7 %copy.7 = f32[16,32,128]{2,1,0:T(8,128)} copy(f32[16,32,128]{2,1,0:T(8,128)S(1)} %get-tuple-element.5) | data formatting | bytes 524288
Async XLA Ops:
  0.6 1.0 %copy-start = (f32[16,32,128]{2,1,0:T(8,128)S(1)}, f32[16,32,128]{2,1,0:T(8,128)}, u32[]{:S(2)}) copy-start(f32[16,32,128]{2,1,0:T(8,128)} %refs_0_.1) | copy-start | bytes 786436
  1.6 0.9 %copy-start.1 = (f32[16,32,128]{2,1,0:T(8,128)S(1)}, f32[16,32,128]{2,1,0:T(8,128)}, u32[]{:S(2)}) copy-start(f32[16,32,128]{2,1,0:T(8,128)} %refs_1_.1) | copy-start | bytes 786436

commit v4 on v3

--- a/solution.py
+++ b/solution.py
@@ -1,3 +1,5 @@
+import functools
+
 import jax
 import jax.numpy as jnp
 from jax import lax
@@ -164,8 +166,9 @@
 
 
 class Margin:
-    def __init__(self, ext, px, left, right, sems, place):
+    def __init__(self, ext, px, left, right, pairs, land, sems, place):
         self.ext, self.px, self.left, self.right = ext, px, left, right
+        self.pairs, self.land = pairs, land
         self.send, self.recv = sems
         self.place = place
         self.copies = []
@@ -179,17 +182,19 @@
             packed = jnp.where(spot & (lane % 16 < 8), shift_lanes(x, 16 * z - 64), packed)
             packed = jnp.where(spot & (lane % 16 >= 8), shift_lanes(x, 16 * z), packed)
         self.px[...] = packed
-        at, size = self.place
+        for z in range(4):
+            first = shift_lanes(self.ext[z, 0:16], -MARGIN)
+            second = shift_lanes(self.ext[z + 4, 0:16], 64 - MARGIN)
+            self.pairs[z] = jnp.where(lane < 64, first, second)
         rows_out = {-1: pl.ds(0, 8), 0: pl.ds(0, 16), 1: pl.ds(8, 8)}
         rows_in = {-1: pl.ds(16, 8), 0: pl.ds(0, 16), 1: pl.ds(24, 8)}
-        planes_in = {-1: pl.ds(8, 8), 0: pl.ds(0, 8), 1: pl.ds(16, 8)}
         block_in = {-1: 1, 0: 0, 1: 2}
         order = sorted(range(26), key=lambda i: sum(map(abs, SIDES[i])))
         for i in order:
             dz, dx, dy = SIDES[i]
             if dy == 0:
-                src = self.ext.at[pl.ds(0, 8), rows_out[dx], :]
-                dst = self.ext.at[planes_in[dz], rows_in[dx], :]
+                src = self.pairs.at[:, rows_out[dx], :]
+                dst = self.land.at[block_in[dz], :, rows_in[dx], :]
             else:
                 land = self.left if dy == 1 else self.right
                 src = self.px.at[rows_out[dx], :]
@@ -222,16 +227,21 @@
             sides = jnp.where(lane % 16 < 8, self.left[block], self.right[block])
             self.left[block] = sides
 
-            def body(i, carry, block=block, low=low, high=high, own=own):
+            def body(j, carry, block=block, low=low, high=high, own=own, half=0):
+                i = j + 4 * half
                 z = 8 * block + i
                 sides = self.left[block]
-                merged = jnp.where(own, self.ext[z], 0.0)
+                middle = shift_lanes(self.land[block, j], MARGIN - 64 * half)
+                if block == 0:
+                    middle = jnp.where(row < 16, self.ext[z], middle)
+                merged = jnp.where(own, middle, 0.0)
                 merged = jnp.where(low, shift_lanes(sides, -16 * i), merged)
                 merged = jnp.where(high, shift_lanes(sides, 64 - 16 * i), merged)
                 self.ext[z] = merged
                 return carry
 
-            loop(8, body, 0)
+            for half in range(2):
+                loop(4, functools.partial(body, half=half), 0)
 
 
 def neighbour(place, dz, dx, dy):
@@ -359,11 +369,12 @@
     loop(planes // 2, body, 0)
 
 
-def kernel(size, names, source_hbm, weight_hbm, out_ref, residual_ref, *scratch):
+def kernel(size, names, source_hbm, weight_hbm, out_hbm, residual_hbm, *scratch):
     ref = dict(zip(names, scratch))
     source_ref, weight_ref = ref["source"], ref["weight"]
     load_weight = pltpu.make_async_copy(weight_hbm, weight_ref, ref["load"].at[0])
     load_source = pltpu.make_async_copy(source_hbm, source_ref, ref["load"].at[1])
+    out_ref, residual_ref = ref["out"], ref["residual"]
     at = {a: lax.axis_index(a) for a in AXES}
     place = (at, size)
 
@@ -391,7 +402,7 @@
     margins = {}
     for k, name in enumerate(("w1", "s1")):
         margins[name] = Margin(
-            *(ref[f"{name}{part}"] for part in ("", "_px", "_left", "_right")),
+            *(ref[f"{name}{part}"] for part in ("", "_px", "_left", "_right", "_pairs", "_land")),
             (ref["send_side"].at[k], ref["recv_side"].at[k]),
             place,
         )
@@ -701,13 +712,24 @@
         return last.put(z, x, carry)
 
     last.start(relax_into(swap, source_ref, faces, rate, put, last.empty()))
+    stores = [pltpu.make_async_copy(out_ref, out_hbm, ref["load"].at[2])]
+    stores[0].start()
     last.finish()
 
     def body(z, carry):
         residual_ref[z] = source_ref[z] - applied(last.around(z), faces, z)
         return carry
 
-    loop(16, body, 0)
+    for half in range(2):
+        lax.fori_loop(8 * half, 8 * half + 8, body, 0, unroll=2)
+        part = pl.ds(8 * half, 8)
+        store = pltpu.make_async_copy(
+            residual_ref.at[part], residual_hbm.at[part], ref["load"].at[3 + half]
+        )
+        store.start()
+        stores.append(store)
+    for store in stores:
+        store.wait()
 
 
 def buffers(size):
@@ -736,11 +758,15 @@
         vmem(f"t{level}", rows, LANES)
     for name in ("w1", "s1"):
         vmem(f"{name}_px", 16, LANES)
+        vmem(f"{name}_pairs", 4, 16, LANES)
+        vmem(f"{name}_land", 3, 4, 32, LANES)
         vmem(f"{name}_left", 3, 32, LANES)
         vmem(f"{name}_right", 3, 32, LANES)
     vmem("s4", 1, 4, LANES)
     vmem("source", 16, 32, LANES)
     vmem("weight", 16, 32, LANES)
+    vmem("out", 16, 32, LANES)
+    vmem("residual", 16, 32, LANES)
     for level, rows in ((2, 8), (3, 4), (4, 2)):
         vmem(f"h{level}", 16 >> level, rows, LANES)
         vmem(f"u{level - 1}", 2 * rows, LANES)
@@ -763,7 +789,7 @@
         vmem(f"g2{kind}", 8, LANES)
         vmem(f"g5{kind}", size["gz"], 8, LANES)
     vmem("g6", size["gx"] * size["gz"], 2 * LANES)
-    shapes["load"] = pltpu.SemaphoreType.DMA((2,))
+    shapes["load"] = pltpu.SemaphoreType.DMA((5,))
     shapes["send"] = pltpu.SemaphoreType.DMA((len(SWAP_FIELDS), 6))
     shapes["recv"] = pltpu.SemaphoreType.DMA((len(SWAP_FIELDS), 6))
     shapes["send_side"] = pltpu.SemaphoreType.DMA((2, 26))
@@ -792,10 +818,10 @@
             run,
             out_shape=(block, block),
             in_specs=[pl.BlockSpec(memory_space=pltpu.HBM)] * 2,
-            out_specs=[pl.BlockSpec(memory_space=pltpu.VMEM)] * 2,
+            out_specs=[pl.BlockSpec(memory_space=pltpu.HBM)] * 2,
             scratch_shapes=list(shapes.values()),
             compiler_params=pltpu.CompilerParams(
-                collective_id=0, has_side_effects=True, vmem_limit_bytes=48 * 1024 * 1024
+                collective_id=0, has_side_effects=True, vmem_limit_bytes=63 * 1024 * 1024
             ),
         )(source, conductivity)
 

time: 65.2 us -> 63.6 us (0.975)
  local copies, waits for them, and re-layouts: 3.3 us -> 2.42 us
  Pallas kernels: 61.1 us -> 60.4 us
    unnamed x6 -> x4, local copies, waits for them, and re-layouts: 3.3 us -> 2.42 us
    pallas_call x1, Pallas kernels: 61.1 us -> 60.4 us  [body(): pl.pallas_call(run, out_shape=(block, block), in_specs=[pl.BlockSpec(memo...]
where the time goes in v4:
time: 63.6 us; the launch traced here: 63.5 us
  Pallas kernels  60.4 us (95%)
  local copies, waits for them, and re-layouts  2.42 us (4%)
  between operations  0.65 us (1%)
    pallas_call x1, Pallas kernels, body(): pl.pallas_call(run, out_shape=(block, block), in_specs=[pl.BlockSpec(memo...  60.4 us
    unnamed x4, local copies, waits for them, and re-layouts  2.42 us

profile of v4, /device:TPU:1, one launch (start us, length us, event | category | flops | bytes accessed | tf_op | source)
XLA Modules:
  0.0 63.5 jit_solution(14264490963573794799)
XLA Ops:
  0.6 60.4 %shard_map.41 = (f32[16,32,128]{2,1,0:T(8,128)}, f32[16,32,128]{2,1,0:T(8,128)}) custom-call(f32[16,32,128]{2,1,0:T(8,128)} %refs_0_.1, f32[16,32,128]{2,1,0:T(8,128)} %refs_1_.1), custom_call_target="tpu_custom_call" | custom-call | tf_op jit(solution)/shard_map/pallas_call | solution.py:817
  61.0 0.0 copy-start
  61.0 1.7 %copy.6 = f32[16,32,128]{2,1,0:T(8,128)} copy(f32[16,32,128]{2,1,0:T(8,128)} %get-tuple-element.4) | data formatting | bytes 524288
  62.8 0.0 copy-done
  62.8 0.7 %copy.7 = f32[16,32,128]{2,1,0:T(8,128)} copy(f32[16,32,128]{2,1,0:T(8,128)S(1)} %copy-done) | data formatting | bytes 524288
Async XLA Ops:
  61.0 1.7 %copy-start = (f32[16,32,128]{2,1,0:T(8,128)S(1)}, f32[16,32,128]{2,1,0:T(8,128)}, u32[]{:S(2)}) copy-start(f32[16,32,128]{2,1,0:T(8,128)} %get-tuple-element.5) | copy-start | bytes 786436

commit v5 on v4

--- a/solution.py
+++ b/solution.py
@@ -38,7 +38,7 @@
         for i in range(count):
             carry = body(i, carry)
         return carry
-    return lax.fori_loop(0, count, body, carry, unroll=2)
+    return lax.fori_loop(0, count, body, carry, unroll=True)
 
 
 def shift_lanes(x, amount):
@@ -721,7 +721,7 @@
         return carry
 
     for half in range(2):
-        lax.fori_loop(8 * half, 8 * half + 8, body, 0, unroll=2)
+        lax.fori_loop(8 * half, 8 * half + 8, body, 0, unroll=8)
         part = pl.ds(8 * half, 8)
         store = pltpu.make_async_copy(
             residual_ref.at[part], residual_hbm.at[part], ref["load"].at[3 + half]

time: 63.6 us -> 55.3 us (0.87)
  Pallas kernels: 60.4 us -> 52 us
    pallas_call x1, Pallas kernels: 60.4 us -> 52 us  [body(): pl.pallas_call(run, out_shape=(block, block), in_specs=[pl.BlockSpec(memo...]
where the time goes in v5:
time: 55.3 us; the launch traced here: 55.1 us
  Pallas kernels  52 us (94%)
  local copies, waits for them, and re-layouts  2.42 us (4%)
  between operations  0.65 us (1%)
    pallas_call x1, Pallas kernels, body(): pl.pallas_call(run, out_shape=(block, block), in_specs=[pl.BlockSpec(memo...  52 us
    unnamed x4, local copies, waits for them, and re-layouts  2.42 us

profile of v5, /device:TPU:1, one launch (start us, length us, event | category | flops | bytes accessed | tf_op | source)
XLA Modules:
  0.0 55.1 jit_solution(3312705069296727741)
XLA Ops:
  0.6 52.0 %shard_map.41 = (f32[16,32,128]{2,1,0:T(8,128)}, f32[16,32,128]{2,1,0:T(8,128)}) custom-call(f32[16,32,128]{2,1,0:T(8,128)} %refs_0_.1, f32[16,32,128]{2,1,0:T(8,128)} %refs_1_.1), custom_call_target="tpu_custom_call" | custom-call | tf_op jit(solution)/shard_map/pallas_call | solution.py:817
  52.7 0.0 copy-start
  52.7 1.7 %copy.6 = f32[16,32,128]{2,1,0:T(8,128)} copy(f32[16,32,128]{2,1,0:T(8,128)} %get-tuple-element.4) | data formatting | bytes 524288
  54.4 0.0 copy-done
  54.4 0.7 %copy.7 = f32[16,32,128]{2,1,0:T(8,128)} copy(f32[16,32,128]{2,1,0:T(8,128)S(1)} %copy-done) | data formatting | bytes 524288
Async XLA Ops:
  52.7 1.7 %copy-start = (f32[16,32,128]{2,1,0:T(8,128)S(1)}, f32[16,32,128]{2,1,0:T(8,128)}, u32[]{:S(2)}) copy-start(f32[16,32,128]{2,1,0:T(8,128)} %get-tuple-element.5) | copy-start | bytes 786436
